TPU v7x, 128 devices: a whole 4x4x4 slice. The times are simulated.
128 devices in a mesh: dp: 8 (over y_lo, z), cent: 16 (over x, y_hi, core).
Axes of the slice: x: 4, y: 4 (y_hi: 2, y_lo: 2; y = y_hi * 2 + y_lo), z: 4, core: 2. Of those that a mesh axis runs over, the one named last changes fastest.
Arguments:
- points: bfloat16 [524288, 1536], P(('dp', 'cent')), may hold values from -8 to 8
- assign: int32 [524288], P(('dp', 'cent')), may hold values from 0 to 2047, as said below
- counts: int32 [2048], P('cent'), may hold values from 1 to 1024, as said below
- level2: bfloat16 [256, 1536], P('cent'), may hold values from -3 to 3
- l2_assign: int32 [2048, 1], P('cent'), may hold values from 0 to 255, as said below
Outputs:
- new_level1: bfloat16 [2048, 1536], P('cent')
- nearest: float32 [2048], P('cent')
- new_level2: bfloat16 [256, 1536], P('cent')
Inputs may be any that keep to these rules, and one draw needn't show every extreme that they name: `assign`: every level-1 centroid is named by at least one point; the points of each level-1 centroid stand in consecutive rows. counts[k] is the number of points of all devices whose assign is k. `l2_assign`: every level-2 centroid is named by at least one row; the owner of level-2 centroid j is j // 16; in each aligned block of 128 rows at most 16 rows name centroids of one owner, and some owner is named exactly that often in every block; the per-owner numbers of rows are, in every block, the same numbers in another order, and the centroids of each owner are named by exactly 128 rows in all.
All inputs are finite; a program needn't handle non-finite values.
Results may differ from a plain program's by a relative error of at most 0.013.
Values may be sent and summed in bfloat16 or wider, within the bound.
No kernel may reach another device: no remote copies, remote signals or barrier semaphores. Data moves between devices by JAX's collectives and lax.ppermute only.
A program may use at most 64 MiB of HBM per device.

v0:
```python
import math

import jax
import jax.numpy as jnp
from jax import lax
from jax.sharding import PartitionSpec as P


def member_sums(points, targets, total_rows):
    block_size = math.gcd(total_rows, 512)

    def one_block(block_index):
        first_row = block_index * block_size
        labels = first_row + lax.iota(jnp.int32, block_size)
        one_hot = (targets[None, :] == labels[:, None]).astype(jnp.bfloat16)
        return jnp.dot(one_hot, points, preferred_element_type=jnp.float32)

    block_sums = lax.map(one_block, jnp.arange(total_rows // block_size, dtype=jnp.int32))
    return block_sums.reshape(total_rows, points.shape[1])


def body(points, assign, counts, level2, l2_assign):
    feature_width = points.shape[1]
    cent_count = lax.axis_size("cent")
    owned_rows = counts.shape[0]
    level1_total = owned_rows * cent_count
    member_counts = counts.astype(jnp.float32)
    partial_sums = member_sums(points, assign, level1_total)
    owned_sums = lax.psum_scatter(
        partial_sums.astype(jnp.bfloat16), "cent", scatter_dimension=0, tiled=True
    ).astype(jnp.float32)
    summed = lax.psum(owned_sums, "dp")
    new_level1 = (summed / member_counts[:, None]).astype(jnp.bfloat16)
    query_float = new_level1.astype(jnp.float32)
    query_norms = jnp.sum(query_float * query_float, axis=1)
    start_value = jnp.full((new_level1.shape[0],), jnp.inf, jnp.float32)
    centre_piece = lax.all_gather(level2, "cent", axis=0, tiled=True)
    centre_float = centre_piece.astype(jnp.float32)
    centre_norms = jnp.sum(centre_float * centre_float, axis=1)
    cross = jnp.einsum("rd,md->rm", new_level1, centre_piece, preferred_element_type=jnp.float32)
    distance = (query_norms[:, None] - 2.0 * cross + centre_norms[None, :]) / feature_width
    nearest_part = jnp.minimum(start_value, jnp.min(distance, axis=1))
    level2_owned = level2.shape[0]
    level2_total = level2_owned * cent_count
    level2_labels = l2_assign[:, 0]
    labels_two = lax.iota(jnp.int32, level2_total)
    one_hot_two = level2_labels[None, :] == labels_two[:, None]
    partial_two = jnp.dot(
        one_hot_two.astype(jnp.bfloat16), new_level1, preferred_element_type=jnp.float32
    )
    partial_members = jnp.sum(one_hot_two.astype(jnp.float32), axis=1)
    sums_two, members_two = (
        lax.psum_scatter(partial_two, "cent", scatter_dimension=0, tiled=True),
        lax.psum_scatter(partial_members, "cent", scatter_dimension=0, tiled=True),
    )
    new_level2 = (sums_two / members_two[:, None]).astype(jnp.bfloat16)
    return (new_level1, nearest_part, new_level2)


def solution(mesh):
    placed = (
        P(("dp", "cent"), None),
        P(("dp", "cent")),
        P("cent"),
        P("cent", None),
        P("cent", None),
    )
    return jax.shard_map(
        body,
        mesh=mesh,
        in_specs=placed,
        out_specs=(P("cent", None), P("cent"), P("cent", None)),
        check_vma=False,
    )
```

profile of v0, /device:TPU:1, one launch (start us, length us, event | category | flops | bytes accessed | tf_op | source)
XLA Modules:
  0.0 265.7 jit_solution(487682137476493075)
XLA Ops:
  7.2 0.0 reduce-scatter.3.cloned.1.call-start
  7.2 47.7 %while.10 = (s32[]{:T(128)}, bf16[4,512,1536]{2,1,0:T(8,128)(2,1)}, s32[4096]{0:T(1024)}, s32[4]{0:T(128)S(1)}, bf16[4096,1536]{1,0:T(8,128)(2,1)}, /*index=5*/s32[]{:T(128)}, s32[1]{0:T(128)}) while((s32[]{:T(128)}, bf16[4,512,1536]{2,1,0:T(8,128)(2,1)}, s32[4096]{0:T(1024)}, s32[4]{0:T(128)S(1)}, bf16[4096,1536]{1,0:T(8,128)(2,1)}, ...), condition=%wide.region_1.2_spmd, body=%wide.region_0.1_spmd.sunk | while | flops 6444548608 | bytes 15749737 | solution.py:18
  7.2 0.6 dynamic_slice.5
  8.5 10.7 %fusion.25 = bf16[4,512,1536]{2,1,0:T(8,128)(2,1)} fusion(bf16[4,512,1536]{2,1,0:T(8,128)(2,1)} %get-tuple-element.82, s32[]{:T(128)} %get-tuple-element.81, bf16[4096,1536]{1,0:T(8,128)(2,1)} %get-tuple-element.92, s32[4096]{0:T(1024)} %get-tuple-element.90, s32[512]{0:T(512)S(1)} %iota_add_fusion.2), kind=kOutput, calls=%fused_computation.5.clone.1 | convolution fusion | flops 6444548096 | bytes 15747584 | tf_op jit(solution)/shard_map/while/body/eval_jaxpr/dot_general | solution.py:16
  19.2 0.6 dynamic_slice.5
  20.4 10.6 %fusion.25 = bf16[4,512,1536]{2,1,0:T(8,128)(2,1)} fusion(bf16[4,512,1536]{2,1,0:T(8,128)(2,1)} %get-tuple-element.82, s32[]{:T(128)} %get-tuple-element.81, bf16[4096,1536]{1,0:T(8,128)(2,1)} %get-tuple-element.92, s32[4096]{0:T(1024)} %get-tuple-element.90, s32[512]{0:T(512)S(1)} %iota_add_fusion.2), kind=kOutput, calls=%fused_computation.5.clone.1 | convolution fusion | flops 6444548096 | bytes 15747584 | tf_op jit(solution)/shard_map/while/body/eval_jaxpr/dot_general | solution.py:16
  31.0 0.6 dynamic_slice.5
  32.3 10.7 %fusion.25 = bf16[4,512,1536]{2,1,0:T(8,128)(2,1)} fusion(bf16[4,512,1536]{2,1,0:T(8,128)(2,1)} %get-tuple-element.82, s32[]{:T(128)} %get-tuple-element.81, bf16[4096,1536]{1,0:T(8,128)(2,1)} %get-tuple-element.92, s32[4096]{0:T(1024)} %get-tuple-element.90, s32[512]{0:T(512)S(1)} %iota_add_fusion.2), kind=kOutput, calls=%fused_computation.5.clone.1 | convolution fusion | flops 6444548096 | bytes 15747584 | tf_op jit(solution)/shard_map/while/body/eval_jaxpr/dot_general | solution.py:16
  42.9 0.6 dynamic_slice.5
  44.2 10.7 %fusion.25 = bf16[4,512,1536]{2,1,0:T(8,128)(2,1)} fusion(bf16[4,512,1536]{2,1,0:T(8,128)(2,1)} %get-tuple-element.82, s32[]{:T(128)} %get-tuple-element.81, bf16[4096,1536]{1,0:T(8,128)(2,1)} %get-tuple-element.92, s32[4096]{0:T(1024)} %get-tuple-element.90, s32[512]{0:T(512)S(1)} %iota_add_fusion.2), kind=kOutput, calls=%fused_computation.5.clone.1 | convolution fusion | flops 6444548096 | bytes 15747584 | tf_op jit(solution)/shard_map/while/body/eval_jaxpr/dot_general | solution.py:16
  54.9 0.0 copy-start.3
  54.9 0.0 copy-start.2
  54.9 0.0 copy-start.4
  54.9 0.0 copy-start.1
  54.9 0.0 reduce-scatter.3.cloned.1.call-update
  54.9 0.0 reduce-scatter.5.cloned.1.call-start
  55.0 0.6 copy-done.3
  55.6 91.1 %reduce-scatter.3.cloned.1.call-done = bf16[128,1536]{1,0:T(8,128)(2,1)} async-done(((bf16[2048,1536]{1,0:T(8,128)(2,1)}), bf16[128,1536]{1,0:T(8,128)(2,1)}) %reduce-scatter.3.cloned.1.call-update) | async-done | bytes 393232 | tf_op jit(solution)/shard_map/reduce_scatter | solution.py:29
  146.6 35.4 %all-reduce.2 = f32[128,1536]{1,0:T(8,128)S(1)} all-reduce(bf16[128,1536]{1,0:T(8,128)(2,1)} %reduce-scatter.3.cloned.1.call-done), channel_id=1, replica_groups=mesh['dp'=8,'cent'=16] {'dp'}, use_global_device_ids=true, to_apply=%region_3.4 | all-reduce | flops 196608 | bytes 1179648 | tf_op jit(solution)/shard_map/psum | solution.py:32
  182.1 0.2 multiply_reduce_fusion.1
  182.3 0.0 copy-start
  182.3 0.0 copy-done.2
  182.3 1.5 fusion.14
  183.9 0.0 reduce-scatter.5.cloned.1.call-update
  183.9 0.0 copy-done.4
  183.9 0.6 dynamic-slice
  185.1 0.1 convert_reduce_fusion
  185.2 40.9 %all-reduce = f32[256]{0:T(256)S(1)} all-reduce(f32[256]{0:T(256)S(1)} %convert_reduce_fusion), channel_id=4, replica_groups=mesh['dp'=8,'cent'=16] {'cent'}, use_global_device_ids=true, to_apply=%region_9.10.clone | all-reduce | flops 256 | bytes 2048
  226.2 0.1 dynamic-slice.1
  226.2 0.0 copy-done.1
  226.2 22.4 %all_gather.3 = bf16[256,1536]{1,0:T(8,128)(2,1)S(1)} all-gather(bf16[16,1536]{1,0:T(8,128)(2,1)S(1)} %copy-done.1), channel_id=1, replica_groups=mesh['dp'=8,'cent'=16] {'cent'}, dimensions={0}, use_global_device_ids=true | all-gather | bytes 835584 | tf_op jit(solution)/shard_map/all_gather | solution.py:37
  248.7 0.2 multiply_reduce_fusion
  248.9 1.0 fusion.13
  249.9 7.4 %reduce-scatter.5.cloned.1.call-done = f32[16,1536]{1,0:T(8,128)} async-done(((f32[256,1536]{1,0:T(8,128)}), f32[16,1536]{1,0:T(8,128)}) %reduce-scatter.5.cloned.1.call-update) | async-done | bytes 98320 | tf_op jit(solution)/shard_map/reduce_scatter | solution.py:53
  257.3 1.6 divide_convert_fusion.1
  258.9 0.0 copy-done
  (7 shorter events, 0.0 us)
Async XLA Ops:
  7.2 139.5 %reduce-scatter.3.cloned.1.call-start = ((), (), s32[]{:S(2)}) async-start(), calls=%async_computation.2 | async-start | bytes 6684672 | tf_op jit(solution)/shard_map/reduce_scatter | solution.py:29
  54.9 0.7 copy-start.3
  54.9 127.4 %copy-start.2 = (s32[128,1]{0,1:T(1,128)S(1)}, s32[128,1]{0,1:T(1,128)}, u32[]{:S(2)}) copy-start(s32[128,1]{0,1:T(1,128)} %param.11) | copy-start | bytes 1540
  54.9 129.0 %copy-start.4 = (u32[128]{0:T(128)S(1)}, u32[128]{0:T(128)}, u32[]{:S(2)}) copy-start(u32[128]{0:T(128)} %constant.25) | copy-start | bytes 1540
  54.9 171.3 %copy-start.1 = (bf16[16,1536]{1,0:T(8,128)(2,1)S(1)}, bf16[16,1536]{1,0:T(8,128)(2,1)}, u32[]{:S(2)}) copy-start(bf16[16,1536]{1,0:T(8,128)(2,1)} %param.10) | copy-start | bytes 147460
  54.9 202.3 %reduce-scatter.5.cloned.1.call-start = ((), (), s32[]{:S(2)}) async-start(), calls=%async_computation.3 | async-start | bytes 1671168 | tf_op jit(solution)/shard_map/reduce_scatter | solution.py:53
  182.3 76.6 %copy-start = (bf16[128,1536]{1,0:T(8,128)(2,1)}, bf16[128,1536]{1,0:T(8,128)(2,1)S(1)}, u32[]{:S(2)}) copy-start(bf16[128,1536]{1,0:T(8,128)(2,1)S(1)} %get-tuple-element.42) | copy-start | bytes 1179652
Sparse Core Ops, SparseCore 0:
  55.1 91.5 reduce-scatter.2
  184.0 73.2 reduce-scatter.4
where the time goes:
time: 267 us; the launch traced here: 266 us
  blocking collectives  98.8 us (37%)
  waiting for transfers between devices  98.5 us (37%)
  matrix products  45.2 us (17%)
  between operations  14.8 us (6%)
  local copies, waits for them, and re-layouts  3.58 us (1%)
    reduce_scatter x1, waiting for transfers between devices, body(): lax.psum_scatter(partial_sums.astype(jnp.bfloat16), 'cent', scatter_dimen...  91.1 us
    dot_general x4, matrix products, one_block(): return jnp.dot(one_hot, points, preferred_element_type=jnp.float32)  42.7 us
    unnamed x1, blocking collectives  40.9 us
    psum x1, blocking collectives, body(): summed = lax.psum(owned_sums, 'dp')  35.4 us
    all_gather x1, blocking collectives, body(): centre_piece = lax.all_gather(level2, 'cent', axis=0, tiled=True)  22.4 us
    reduce_scatter x1, waiting for transfers between devices, body(): lax.psum_scatter(partial_two, 'cent', scatter_dimension=0, tiled=True)  7.38 us
  transfers between devices with their start and end apart: 2, of which 2 were waited for; matrix products, arithmetic and copies ran while one was open for 1% of the time, Pallas kernels for 0%

commit v1 on v0

v1 whole, which is shorter than its diff:
```python
import jax
import jax.numpy as jnp
from jax import lax
from jax.experimental import pallas as pl
from jax.experimental.pallas import tpu as pltpu
from jax.sharding import PartitionSpec as P

BOTH = ("dp", "cent")
F32 = jnp.float32
BF16 = jnp.bfloat16
SLOTS = 32
LANES = 128
FIELDS = 16
COLS = 12
BLOCK = 512


def nt_dot(left, right):
    return lax.dot_general(left, right, (((1,), (1,)), ((), ())), preferred_element_type=F32)


def iota(shape, axis):
    return lax.broadcasted_iota(jnp.int32, shape, axis)


def run_sums_kernel(first_slot, *refs):
    if first_slot is None:
        slot_ref, *refs = refs
        first = slot_ref[0].astype(F32)
    else:
        first = float(first_slot)
    assign_ref, counts_ref, label_ref, points_ref, out_ref, rank_ref, acc_ref, id_ref, fields_ref, turned_ref = refs
    step = pl.program_id(0)
    rows_per = BLOCK // LANES
    steps = pl.num_programs(0)
    total_rows = assign_ref.shape[0]

    @pl.when(step == 0)
    def _():
        assign = assign_ref[...]
        row, lane = iota(assign.shape, 0), iota(assign.shape, 1)
        shifted = pltpu.roll(assign, 1, 1)
        before = jnp.where(lane == 0, pltpu.roll(shifted, 1, 0), shifted)
        starts = (assign != before) | ((row == 0) & (lane == 0))
        starts_f = jnp.where(starts, 1.0, 0.0)
        upper = jnp.where(iota((LANES, LANES), 0) <= iota((LANES, LANES), 1), 1.0, 0.0).astype(BF16)
        inner = jnp.dot(starts_f.astype(BF16), upper, preferred_element_type=F32)
        row_total = jnp.broadcast_to(inner[:, LANES - 1 :], inner.shape).astype(BF16)
        lower = jnp.where(iota((total_rows, total_rows), 1) < iota((total_rows, total_rows), 0), 1.0, 0.0)
        rank = inner + jnp.dot(lower.astype(BF16), row_total, preferred_element_type=F32) - 1.0
        rounds = (rank[total_rows - 1 :, LANES - 1 :].astype(jnp.int32) + SLOTS) // SLOTS
        rank = rank - first
        slot = iota((SLOTS, LANES), 0).astype(F32)
        named = jnp.where(starts, assign, 0).astype(F32)
        found = jnp.zeros((SLOTS, LANES), F32)
        for q in range(total_rows):
            rank_ref[q // rows_per, q % rows_per : q % rows_per + 1, :] = rank[q : q + 1, :]
            found = found + jnp.where(rank[q : q + 1, :] == slot, named[q : q + 1, :], 0.0)
        ids = jnp.broadcast_to(jnp.sum(found, axis=1, keepdims=True).astype(jnp.int32), (SLOTS, LANES))
        id_ref[...] = ids
        own = lax.axis_index("dp") * 16
        pick = iota((16, LANES), 1) == iota((16, LANES), 0) + own
        def picked(values):
            return jnp.broadcast_to(jnp.sum(jnp.where(pick, values, 0.0), axis=1, keepdims=True), (16, LANES))
        count = counts_ref[...]
        fields_ref[pl.ds(14, 16, stride=FIELDS), :] = picked(label_ref[...].astype(F32))
        fields_ref[pl.ds(14 + 16 * FIELDS, 16, stride=FIELDS), :] = picked((count // 256).astype(F32))
        fields_ref[pl.ds(15, 16, stride=FIELDS), :] = picked((count % 256).astype(F32))
        fields_ref[pl.ds(15 + 16 * FIELDS, 16, stride=FIELDS), :] = jnp.broadcast_to(rounds.astype(F32), (16, LANES))
        fields_ref[pl.ds(12, SLOTS, stride=FIELDS), :] = (ids // LANES).astype(F32)
        fields_ref[pl.ds(13, SLOTS, stride=FIELDS), :] = (ids % LANES).astype(F32)
        acc_ref[...] = jnp.zeros_like(acc_ref)

    slot = iota((SLOTS, LANES), 0).astype(F32)
    ranks = rank_ref[step]
    one_hot = jnp.concatenate(
        [jnp.where(ranks[q : q + 1, :] == slot, 1.0, 0.0).astype(BF16) for q in range(rows_per)], axis=1
    )
    acc_ref[...] += jnp.dot(one_hot, points_ref[...], preferred_element_type=F32)

    @pl.when(step == steps - 1)
    def _():
        for f in range(COLS):
            fields_ref[pl.ds(f, SLOTS, stride=FIELDS), :] = acc_ref[:, f * LANES : (f + 1) * LANES]
        for q in range(4):
            turned_ref[pl.ds(q, LANES, stride=4), :] = fields_ref[q * LANES : (q + 1) * LANES, :].T
        out_ref[...] = turned_ref[...].astype(BF16).reshape(LANES, 4, LANES)


def run_sums(points, assign, counts, labels, first_slot):
    rows, width = points.shape
    whole = lambda shape: pl.BlockSpec(shape, lambda i: (0,) * len(shape))
    static = isinstance(first_slot, int)
    specs = [
        whole((rows // LANES, LANES)),
        whole((1, LANES)),
        whole((1, LANES)),
        pl.BlockSpec((BLOCK, width), lambda i: (i, 0)),
    ]
    args = [assign, counts, labels, points]
    if not static:
        specs = [pl.BlockSpec(memory_space=pltpu.SMEM)] + specs
        args = [first_slot] + args

    def kernel(*refs):
        run_sums_kernel(first_slot if static else None, *refs)

    return pl.pallas_call(
        kernel,
        grid=(rows // BLOCK,),
        in_specs=specs,
        out_specs=whole((LANES, 4, LANES)),
        out_shape=jax.ShapeDtypeStruct((LANES, 4, LANES), BF16),
        scratch_shapes=[
            pltpu.VMEM((rows // BLOCK, BLOCK // LANES, LANES), F32),
            pltpu.VMEM((SLOTS, width), F32),
            pltpu.VMEM((SLOTS, LANES), jnp.int32),
            pltpu.VMEM((SLOTS * FIELDS, LANES), F32),
            pltpu.VMEM((SLOTS * FIELDS, LANES), F32),
        ],
        cost_estimate=pl.CostEstimate(
            flops=2 * 256 * rows * width, bytes_accessed=rows * width * 2, transcendentals=0
        ),
        compiler_params=pltpu.CompilerParams(vmem_limit_bytes=12 << 20),
        name="run_sums",
    )(*args)


def means_kernel(carried, *refs):
    if carried:
        runs_ref, before_ref, *refs = refs
    else:
        runs_ref, *refs = refs
    out_ref, acc_ref, rounds_ref, wide_ref, field_ref, send_ref = refs
    wide_ref[...] = runs_ref[...].reshape(4 * LANES, LANES).astype(F32)
    for q in range(4):
        field_ref[q * LANES : (q + 1) * LANES, :] = wide_ref[pl.ds(q, LANES, stride=4), :].T
    low_id = iota((LANES, LANES), 0).astype(F32)
    high_id = iota((16, LANES), 0).astype(F32)
    acc = before_ref[...] if carried else None
    for pair in range(SLOTS // 2):
        lefts, rights = [], []
        for r in (2 * pair, 2 * pair + 1):
            block = field_ref[r * FIELDS : (r + 1) * FIELDS, :]
            high = jnp.where(block[12:13, :] == high_id, 1.0, 0.0)
            rights.append(jnp.where(block[13:14, :] == low_id, 1.0, 0.0).astype(BF16))
            lefts.append(
                jnp.concatenate([(high[a : a + 1, :] * block).astype(BF16) for a in range(16)], axis=0)
            )
        part = nt_dot(jnp.concatenate(lefts, axis=1), jnp.concatenate(rights, axis=1))
        acc = part if acc is None else acc + part
    acc_ref[...] = acc

    device = iota((LANES, LANES), 1)
    same_dp = (device // 16) == (iota((LANES, LANES), 0) // 16)
    spread = []
    for first in (14, 14 + 16 * FIELDS, 15):
        value = field_ref[pl.ds(first, 16, stride=FIELDS), :]
        spread.append(jnp.where(same_dp, jnp.concatenate([value] * 8, axis=0), 0.0).astype(BF16))
    owner = jnp.where(iota((16, LANES), 1) % 16 == iota((16, LANES), 0), 1.0, 0.0).astype(BF16)
    numbers = nt_dot(owner, jnp.concatenate(spread, axis=0))
    label = numbers[:, :LANES].astype(jnp.int32)
    count = numbers[:, LANES : 2 * LANES] * 256.0 + numbers[:, 2 * LANES :]
    rounds = jnp.max(field_ref[15 + 16 * FIELDS : 16 + 16 * FIELDS, :])
    rounds_ref[0] = rounds.astype(jnp.int32)

    sums_two = jnp.zeros((16, COLS * 16), F32)
    members = jnp.zeros((16, 16), F32)
    for pair in range(8):
        owners, insides, values = [], [], []
        for a in (2 * pair, 2 * pair + 1):
            mean = (acc[a * 16 : (a + 1) * 16, :] / count[a : a + 1, :]).astype(BF16).astype(F32)
            send_ref[a * 16 : (a + 1) * 16, :] = mean
            own = label[a : a + 1, :]
            owners.append(jnp.where(own // 16 == iota((16, LANES), 0), 1.0, 0.0).astype(BF16))
            inside = jnp.where(own % 16 == iota((16, LANES), 0), 1.0, 0.0)
            insides.append(inside.astype(BF16))
            values.append(
                jnp.concatenate([(inside * mean[f : f + 1, :]).astype(BF16) for f in range(COLS)], axis=0)
            )
        left = jnp.concatenate(owners, axis=1)
        sums_two = sums_two + nt_dot(left, jnp.concatenate(values, axis=1))
        members = members + nt_dot(left, jnp.concatenate(insides, axis=1))
    repeat = jnp.where(iota((16, COLS * 16), 1) % 16 == iota((16, COLS * 16), 0), 1.0, 0.0).astype(BF16)
    members_wide = jnp.dot(members.astype(BF16), repeat, preferred_element_type=F32)
    level2 = sums_two / members_wide
    send_ref[pl.ds(12, 16, stride=16), :] = level2[:, :LANES]
    send_ref[pl.ds(13, 16, stride=16), :] = jnp.concatenate(
        [level2[:, LANES:], jnp.zeros((16, 2 * LANES - COLS * 16), F32)], axis=1
    )
    block = send_ref[...].astype(BF16).reshape(16, 16, LANES)
    for i in range(8):
        out_ref[i * 16 : (i + 1) * 16] = block


def means(runs, before=None):
    vmem = pl.BlockSpec(memory_space=pltpu.VMEM)
    args = [runs] if before is None else [runs, before]

    def kernel(*refs):
        means_kernel(before is not None, *refs)

    return pl.pallas_call(
        kernel,
        in_specs=[vmem] * len(args),
        out_specs=[vmem, vmem, pl.BlockSpec(memory_space=pltpu.SMEM)],
        out_shape=[
            jax.ShapeDtypeStruct((LANES, 16, LANES), BF16),
            jax.ShapeDtypeStruct((16 * FIELDS, LANES), F32),
            jax.ShapeDtypeStruct((1,), jnp.int32),
        ],
        scratch_shapes=[
            pltpu.VMEM((4 * LANES, LANES), F32),
            pltpu.VMEM((4 * LANES, LANES), F32),
            pltpu.VMEM((16 * FIELDS, LANES), F32),
        ],
        compiler_params=pltpu.CompilerParams(vmem_limit_bytes=8 << 20),
        name="means",
    )(*args)


def finish_kernel(parts, rows_ref, *refs):
    centre_refs, (level1_ref, nearest_ref, level2_ref, wide_ref) = refs[:parts], refs[parts:]
    wide_ref[...] = rows_ref[...].reshape(LANES * 16, LANES).astype(F32)
    width = COLS * LANES
    crosses = [None] * parts
    norm = jnp.zeros((1, LANES), F32)
    for f in range(COLS):
        columns = slice(f * LANES, (f + 1) * LANES)
        block = wide_ref[pl.ds(f, LANES, stride=16), :]
        level1_ref[:, columns] = block.T.astype(BF16)
        norm = norm + jnp.sum(block * block, axis=0, keepdims=True)
        small = block.astype(BF16)
        for p in range(parts):
            part = jnp.dot(centre_refs[p][:, columns], small, preferred_element_type=F32)
            crosses[p] = part if crosses[p] is None else crosses[p] + part
    best = None
    for p in range(parts):
        centre = centre_refs[p][...].astype(F32)
        centre_norm = jnp.sum(centre * centre, axis=1, keepdims=True)
        distance = (norm - 2.0 * crosses[p] + centre_norm) / width
        least = jnp.min(distance, axis=0, keepdims=True)
        best = least if best is None else jnp.minimum(best, least)
    nearest_ref[...] = best
    for half in range(2):
        block = wide_ref[pl.ds(12 + half, LANES, stride=16), :].T
        for f in range(8 * half, min(COLS, 8 * half + 8)):
            level2_ref[:, f * LANES : (f + 1) * LANES] = block[(f % 8) * 16 : (f % 8 + 1) * 16, :].astype(BF16)


def finish(rows, centres):
    vmem = pl.BlockSpec(memory_space=pltpu.VMEM)

    def kernel(*refs):
        finish_kernel(len(centres), *refs)

    return pl.pallas_call(
        kernel,
        in_specs=[vmem] * (1 + len(centres)),
        out_specs=[vmem] * 3,
        out_shape=[
            jax.ShapeDtypeStruct((LANES, COLS * LANES), BF16),
            jax.ShapeDtypeStruct((1, LANES), F32),
            jax.ShapeDtypeStruct((16, COLS * LANES), BF16),
        ],
        scratch_shapes=[pltpu.VMEM((LANES * 16, LANES), F32)],
        compiler_params=pltpu.CompilerParams(vmem_limit_bytes=8 << 20),
        name="finish",
    )(rows, *centres)


def exchange(value):
    return lax.all_to_all(value, BOTH, 0, 0, tiled=True)


def swapped(value, mask):
    return lax.ppermute(value, "cent", [(i, i ^ mask) for i in range(16)])


def body(points, assign, counts, level2, l2_assign):
    assign = assign.reshape(-1, LANES)
    counts = counts.reshape(1, LANES)
    labels = l2_assign.reshape(1, LANES)
    near = jnp.concatenate([level2] + [swapped(level2, mask) for mask in (1, 2, 3)], axis=0)
    sums = run_sums(points, assign, counts, labels, 0)
    centres = [near] + [swapped(near, mask) for mask in (4, 8, 12)]
    send, acc, rounds = means(exchange(sums))

    def more(state):
        index, _, acc = state
        sums = run_sums(points, assign, counts, labels, (index * SLOTS).reshape(1))
        send, acc, _ = means(exchange(sums), acc)
        return index + 1, send, acc

    _, send, _ = lax.while_loop(lambda state: state[0] < rounds[0], more, (jnp.int32(1), send, acc))
    new_level1, nearest, new_level2 = finish(exchange(send), centres)
    return new_level1, nearest.reshape(-1), new_level2


def solution(mesh):
    placed = (
        P(("dp", "cent"), None),
        P(("dp", "cent")),
        P("cent"),
        P("cent", None),
        P("cent", None),
    )
    return jax.shard_map(
        body,
        mesh=mesh,
        in_specs=placed,
        out_specs=(P("cent", None), P("cent"), P("cent", None)),
        check_vma=False,
    )
```

time: 267 us -> 60.9 us (0.23)
  blocking collectives: 98.8 us -> 0 us
  waiting for transfers between devices: 98.5 us -> 23 us
  matrix products: 45.2 us -> 0 us
  starting transfers between devices: 0.08 us -> 22.8 us
  between operations: 14.8 us -> 0.78 us
  Pallas kernels: 0 us -> 13.5 us
  local copies, waits for them, and re-layouts: 3.58 us -> 0.04 us
    reduce_scatter x2 -> x0, waiting for transfers between devices: 98.5 us -> none  [the longest x1 91.1 us: body(): lax.psum_scatter(partial_sums.astype(jnp.bfloat16), 'cent', scatter_dimen...]
    dot_general x6 -> x0, matrix products: 45.2 us -> none  [the longest x4 42.7 us: one_block(): return jnp.dot(one_hot, points, preferred_element_type=jnp.float32)]
    unnamed x1 -> x0, blocking collectives: 40.9 us -> none
    psum x1 -> x0, blocking collectives: 35.4 us -> none  [body(): summed = lax.psum(owned_sums, 'dp')]
    all_gather x1 -> x0, blocking collectives: 22.4 us -> none  [body(): centre_piece = lax.all_gather(level2, 'cent', axis=0, tiled=True)]
    all_to_all x0 -> x2, starting transfers between devices: none -> 14.1 us  [exchange(): return lax.all_to_all(value, BOTH, 0, 0, tiled=True)]
    pallas_call x0 -> x3, Pallas kernels: none -> 13.5 us  [the longest x1 9.34 us: run_sums(): pl.pallas_call(kernel, grid=(rows // BLOCK,), in_specs=specs, out_specs=w...]
    ppermute x0 -> x6, waiting for transfers between devices: none -> 13.1 us  [swapped(): return lax.ppermute(value, 'cent', [(i, i ^ mask) for i in range(16)])]
  transfers between devices with their start and end apart: 2 -> 8, of which waited for: 2 -> 3; matrix products, arithmetic and copies ran while one was open for 1% -> 0% of each run, Pallas kernels for 0% -> 20%
where the time goes in v1:
time: 60.9 us; the launch traced here: 60.6 us
  waiting for transfers between devices  23 us (38%)
  starting transfers between devices  22.8 us (37%)
  Pallas kernels  13.5 us (22%)
  between operations  0.78 us (1%)
  loops' own time  0.65 us (1%)
    all_to_all x2, starting transfers between devices, exchange(): return lax.all_to_all(value, BOTH, 0, 0, tiled=True)  14.1 us
    ppermute x6, waiting for transfers between devices, swapped(): return lax.ppermute(value, 'cent', [(i, i ^ mask) for i in range(16)])  13.1 us
    all_to_all x2, waiting for transfers between devices, exchange(): return lax.all_to_all(value, BOTH, 0, 0, tiled=True)  9.91 us
    pallas_call x1, Pallas kernels, run_sums(): pl.pallas_call(kernel, grid=(rows // BLOCK,), in_specs=specs, out_specs=w...  9.34 us
    ppermute x6, starting transfers between devices, swapped(): return lax.ppermute(value, 'cent', [(i, i ^ mask) for i in range(16)])  8.69 us
    pallas_call x1, Pallas kernels, means(): pl.pallas_call(kernel, in_specs=[vmem] * len(args), out_specs=[vmem, vmem...  2.58 us
    pallas_call x1, Pallas kernels, finish(): pl.pallas_call(kernel, in_specs=[vmem] * (1 + len(centres)), out_specs=[v...  1.53 us
  transfers between devices with their start and end apart: 8, of which 3 were waited for; matrix products, arithmetic and copies ran while one was open for 0% of the time, Pallas kernels for 20%

profile of v1, /device:TPU:1, one launch (start us, length us, event | category | flops | bytes accessed | tf_op | source)
XLA Modules:
  0.0 60.6 jit_solution(375985519629371746)
XLA Ops:
  0.6 0.0 copy-start.1
  0.6 0.0 copy-start
  0.7 0.0 copy-start.2
  0.7 0.0 copy-start.3
  0.7 1.5 %collective-permute-start = (bf16[16,1536]{1,0:T(8,128)(2,1)}, bf16[16,1536]{1,0:T(8,128)(2,1)S(1)}, u32[]{:S(2)}, u32[]{:S(2)}) collective-permute-start(bf16[16,1536]{1,0:T(8,128)(2,1)} %param.10), channel_id=1, source_target_pairs={{0,1},{1,0},{2,3},{3,2},{4,5},{5,4},{6,7},{7,6},{8,9},{9,8},{10,11... | collective-permute-start | bytes 147464 | tf_op jit(solution)/shard_map/ppermute | solution.py:277
  2.2 3.0 %collective-permute-start.1 = (bf16[16,1536]{1,0:T(8,128)(2,1)}, bf16[16,1536]{1,0:T(8,128)(2,1)S(1)}, u32[]{:S(2)}, u32[]{:S(2)}) collective-permute-start(bf16[16,1536]{1,0:T(8,128)(2,1)} %param.10), channel_id=1, source_target_pairs={{0,2},{1,3},{2,0},{3,1},{4,6},{5,7},{6,4},{7,5},{8,10},{9,11},{10,... | collective-permute-start | bytes 147464 | tf_op jit(solution)/shard_map/ppermute | solution.py:277
  5.2 0.2 collective-permute-start.2
  5.4 9.3 %run_sums.2 = bf16[128,4,128]{2,1,0:T(4,128)(2,1)} custom-call(s32[32,128]{1,0:T(8,128)} %bitcast.9, s32[1,128]{1,0:T(1,128)} %bitcast.11, s32[1,128]{1,0:T(1,128)} %bitcast.13, bf16[4096,1536]{1,0:T(8,128)(2,1)} %refs_3_.1), custom_call_target="tpu_custom_call" | custom-call | flops 3221225472 | bytes 12582912 | tf_op jit(solution)/shard_map/run_sums/pallas_call | solution.py:108
  14.7 0.0 copy-done.1
  14.8 10.2 %all-to-all-start.1 = ((bf16[128,4,128]{2,1,0:T(4,128)(2,1)}), bf16[128,4,128]{2,1,0:T(4,128)(2,1)S(1)}, u32[]{:S(2)}, u32[]{:S(2)}) async-start(bf16[128,4,128]{2,1,0:T(4,128)(2,1)} %run_sums.2), calls=%async_computation.1 | async-start | bytes 262144 | tf_op jit(solution)/shard_map/all_to_all | solution.py:273
  25.0 0.0 collective-permute-done
  25.0 9.9 %all-to-all-done.1.refs_0_ = bf16[128,4,128]{2,1,0:T(4,128)(2,1)S(1)} async-done(((bf16[128,4,128]{2,1,0:T(4,128)(2,1)}), bf16[128,4,128]{2,1,0:T(4,128)(2,1)S(1)}, u32[]{:S(2)}, u32[]{:S(2)}) %all-to-all-start.1) | async-done | bytes 131104 | tf_op jit(solution)/shard_map/all_to_all | solution.py:273
  34.9 2.6 %means.2 = (bf16[128,16,128]{2,1,0:T(8,128)(2,1)}, f32[256,128]{1,0:T(8,128)S(1)}, s32[1]{0:T(128)}) custom-call(bf16[128,4,128]{2,1,0:T(4,128)(2,1)S(1)} %all-to-all-done.1.refs_0_), custom_call_target="tpu_custom_call" | custom-call | tf_op jit(solution)/shard_map/means/pallas_call | solution.py:203
  37.5 0.0 copy-done
  37.5 0.0 copy-done.2
  37.5 0.0 copy-done.3
  37.6 0.7 %while.12 = (s32[]{:T(128)}, bf16[128,16,128]{2,1,0:T(8,128)(2,1)}, f32[256,128]{1,0:T(8,128)S(1)}, s32[1]{0:T(128)}, s32[32,128]{1,0:T(8,128)S(1)}, /*index=5*/...) while((s32[]{:T(128)}, bf16[128,16,128]{2,1,0:T(8,128)(2,1)}, ...), condition=%wide.region_1.0_spmd, body=%wide.region_0.0_spmd.sunk | while | flops 3221225472 | bytes 13238417 | solution.py:295
  38.2 3.8 %all-to-all-start.2 = ((bf16[128,16,128]{2,1,0:T(8,128)(2,1)}), bf16[128,16,128]{2,1,0:T(8,128)(2,1)S(1)}, u32[]{:S(2)}, u32[]{:S(2)}) async-start(bf16[128,16,128]{2,1,0:T(8,128)(2,1)} %get-tuple-element.56), calls=%async_computation.2 | async-start | bytes 1048576 | tf_op jit(solution)/shard_map/all_to_all | solution.py:273
  42.0 0.0 collective-permute-done.1
  42.1 0.0 collective-permute-done.2
  42.1 1.5 %collective-permute-start.3 = (bf16[64,1536]{1,0:T(8,128)(2,1)S(1)}, bf16[64,1536]{1,0:T(8,128)(2,1)S(1)}, u32[]{:S(2)}, u32[]{:S(2)}) collective-permute-start(bf16[64,1536]{1,0:T(8,128)(2,1)S(1)} %constant_dynamic-update-slice_fusion.refs_1_), channel_id=1, source_target_pairs={{0,4},{1,5},{2,6},{3,7},{4,0},{5,1},{6,2},{7,3},{8,12},{9,13},{10,... | collective-permute-start | bytes 589832 | tf_op jit(solution)/shard_map/ppermute | solution.py:277
  43.6 2.4 %collective-permute-start.4 = (bf16[64,1536]{1,0:T(8,128)(2,1)S(1)}, bf16[64,1536]{1,0:T(8,128)(2,1)S(1)}, u32[]{:S(2)}, u32[]{:S(2)}) collective-permute-start(bf16[64,1536]{1,0:T(8,128)(2,1)S(1)} %constant_dynamic-update-slice_fusion.refs_1_), channel_id=1, source_target_pairs={{0,8},{1,9},{2,10},{3,11},{4,12},{5,13},{6,14},{7,15},{8,0},{9,1},... | collective-permute-start | bytes 589832 | tf_op jit(solution)/shard_map/ppermute | solution.py:277
  46.0 0.1 collective-permute-start.5
  46.1 7.3 %collective-permute-done.3.refs_2_ = bf16[64,1536]{1,0:T(8,128)(2,1)S(1)} collective-permute-done((bf16[64,1536]{1,0:T(8,128)(2,1)S(1)}, bf16[64,1536]{1,0:T(8,128)(2,1)S(1)}, u32[]{:S(2)}, u32[]{:S(2)}) %collective-permute-start.3) | collective-permute-done | bytes 196640 | tf_op jit(solution)/shard_map/ppermute | solution.py:277
  53.4 5.7 %collective-permute-done.4.refs_3_ = bf16[64,1536]{1,0:T(8,128)(2,1)S(1)} collective-permute-done((bf16[64,1536]{1,0:T(8,128)(2,1)S(1)}, bf16[64,1536]{1,0:T(8,128)(2,1)S(1)}, u32[]{:S(2)}, u32[]{:S(2)}) %collective-permute-start.4) | collective-permute-done | bytes 196640 | tf_op jit(solution)/shard_map/ppermute | solution.py:277
  59.1 0.0 collective-permute-done.5.refs_4_
  59.1 0.0 all-to-all-done.2.refs_0_
  59.1 1.5 %finish.1 = (bf16[128,1536]{1,0:T(8,128)(2,1)}, f32[1,128]{1,0:T(1,128)}, bf16[16,1536]{1,0:T(8,128)(2,1)}) custom-call(bf16[128,16,128]{2,1,0:T(8,128)(2,1)S(1)} %all-to-all-done.2.refs_0_, bf16[64,1536]{1,0:T(8,128)(2,1)S(1)} %constant_dynamic-update-slice_fusion.refs_1_, bf16[64,1536]{1,0:T(8,128)(2,1)S(1)} %collective-permute-done.3.refs_2_, ...), custom_call_target="tpu_custom_call" | custom-call | tf_op jit(solution)/shard_map/finish/pallas_call | solution.py:257
  (4 shorter events, 0.0 us)
Async XLA Ops:
  0.6 14.1 %copy-start.1 = (bf16[16,1536]{1,0:T(8,128)(2,1)S(1)}, bf16[16,1536]{1,0:T(8,128)(2,1)}, u32[]{:S(2)}) copy-start(bf16[16,1536]{1,0:T(8,128)(2,1)} %param.10) | copy-start | bytes 147460
  0.6 36.9 %copy-start = (s32[4096]{0:T(1024)S(1)}, s32[4096]{0:T(1024)}, u32[]{:S(2)}) copy-start(s32[4096]{0:T(1024)} %param.8) | copy-start | bytes 49156
  0.7 36.9 %copy-start.2 = (s32[128]{0:T(128)S(1)}, s32[128]{0:T(128)}, u32[]{:S(2)}) copy-start(s32[128]{0:T(128)} %param.9) | copy-start | bytes 1540
  0.7 36.9 %copy-start.3 = (s32[128,1]{0,1:T(1,128)S(1)}, s32[128,1]{0,1:T(1,128)}, u32[]{:S(2)}) copy-start(s32[128,1]{0,1:T(1,128)} %param.11) | copy-start | bytes 1540
  0.7 24.3 %collective-permute-start = (bf16[16,1536]{1,0:T(8,128)(2,1)}, bf16[16,1536]{1,0:T(8,128)(2,1)S(1)}, u32[]{:S(2)}, u32[]{:S(2)}) collective-permute-start(bf16[16,1536]{1,0:T(8,128)(2,1)} %param.10), channel_id=1, source_target_pairs={{0,1},{1,0},{2,3},{3,2},{4,5},{5,4},{6,7},{7,6},{8,9},{9,8},{10,11... | collective-permute-start | bytes 147464 | tf_op jit(solution)/shard_map/ppermute | solution.py:277
  2.2 39.9 %collective-permute-start.1 = (bf16[16,1536]{1,0:T(8,128)(2,1)}, bf16[16,1536]{1,0:T(8,128)(2,1)S(1)}, u32[]{:S(2)}, u32[]{:S(2)}) collective-permute-start(bf16[16,1536]{1,0:T(8,128)(2,1)} %param.10), channel_id=1, source_target_pairs={{0,2},{1,3},{2,0},{3,1},{4,6},{5,7},{6,4},{7,5},{8,10},{9,11},{10,... | collective-permute-start | bytes 147464 | tf_op jit(solution)/shard_map/ppermute | solution.py:277
  5.2 36.9 %collective-permute-start.2 = (bf16[16,1536]{1,0:T(8,128)(2,1)}, bf16[16,1536]{1,0:T(8,128)(2,1)S(1)}, u32[]{:S(2)}, u32[]{:S(2)}) collective-permute-start(bf16[16,1536]{1,0:T(8,128)(2,1)} %param.10), channel_id=1, source_target_pairs={{0,3},{1,2},{2,1},{3,0},{4,7},{5,6},{6,5},{7,4},{8,11},{9,10},{10,... | collective-permute-start | bytes 147464 | tf_op jit(solution)/shard_map/ppermute | solution.py:277
  14.8 20.2 %all-to-all-start.1 = ((bf16[128,4,128]{2,1,0:T(4,128)(2,1)}), bf16[128,4,128]{2,1,0:T(4,128)(2,1)S(1)}, u32[]{:S(2)}, u32[]{:S(2)}) async-start(bf16[128,4,128]{2,1,0:T(4,128)(2,1)} %run_sums.2), calls=%async_computation.1 | async-start | bytes 262144 | tf_op jit(solution)/shard_map/all_to_all | solution.py:273
  38.2 20.9 %all-to-all-start.2 = ((bf16[128,16,128]{2,1,0:T(8,128)(2,1)}), bf16[128,16,128]{2,1,0:T(8,128)(2,1)S(1)}, u32[]{:S(2)}, u32[]{:S(2)}) async-start(bf16[128,16,128]{2,1,0:T(8,128)(2,1)} %get-tuple-element.56), calls=%async_computation.2 | async-start | bytes 1048576 | tf_op jit(solution)/shard_map/all_to_all | solution.py:273
  42.1 11.3 %collective-permute-start.3 = (bf16[64,1536]{1,0:T(8,128)(2,1)S(1)}, bf16[64,1536]{1,0:T(8,128)(2,1)S(1)}, u32[]{:S(2)}, u32[]{:S(2)}) collective-permute-start(bf16[64,1536]{1,0:T(8,128)(2,1)S(1)} %constant_dynamic-update-slice_fusion.refs_1_), channel_id=1, source_target_pairs={{0,4},{1,5},{2,6},{3,7},{4,0},{5,1},{6,2},{7,3},{8,12},{9,13},{10,... | collective-permute-start | bytes 589832 | tf_op jit(solution)/shard_map/ppermute | solution.py:277
  43.6 15.5 %collective-permute-start.4 = (bf16[64,1536]{1,0:T(8,128)(2,1)S(1)}, bf16[64,1536]{1,0:T(8,128)(2,1)S(1)}, u32[]{:S(2)}, u32[]{:S(2)}) collective-permute-start(bf16[64,1536]{1,0:T(8,128)(2,1)S(1)} %constant_dynamic-update-slice_fusion.refs_1_), channel_id=1, source_target_pairs={{0,8},{1,9},{2,10},{3,11},{4,12},{5,13},{6,14},{7,15},{8,0},{9,1},... | collective-permute-start | bytes 589832 | tf_op jit(solution)/shard_map/ppermute | solution.py:277
  46.0 13.1 %collective-permute-start.5 = (bf16[64,1536]{1,0:T(8,128)(2,1)S(1)}, bf16[64,1536]{1,0:T(8,128)(2,1)S(1)}, u32[]{:S(2)}, u32[]{:S(2)}) collective-permute-start(bf16[64,1536]{1,0:T(8,128)(2,1)S(1)} %constant_dynamic-update-slice_fusion.refs_1_), channel_id=1, source_target_pairs={{0,12},{1,13},{2,14},{3,15},{4,8},{5,9},{6,10},{7,11},{8,4},{9,5},... | collective-permute-start | bytes 589832 | tf_op jit(solution)/shard_map/ppermute | solution.py:277

commit v2 on v1

--- a/solution.py
+++ b/solution.py
@@ -12,7 +12,7 @@
 LANES = 128
 FIELDS = 16
 COLS = 12
-BLOCK = 512
+BLOCK = 256
 
 
 def nt_dot(left, right):
@@ -29,74 +29,71 @@
         first = slot_ref[0].astype(F32)
     else:
         first = float(first_slot)
-    assign_ref, counts_ref, label_ref, points_ref, out_ref, rank_ref, acc_ref, id_ref, fields_ref, turned_ref = refs
-    step = pl.program_id(0)
-    rows_per = BLOCK // LANES
-    steps = pl.num_programs(0)
+    assign_ref, counts_ref, label_ref, points_ref, out_ref, held_ref, fields_ref, turned_ref, arrived = refs
     total_rows = assign_ref.shape[0]
-
-    @pl.when(step == 0)
-    def _():
-        assign = assign_ref[...]
-        row, lane = iota(assign.shape, 0), iota(assign.shape, 1)
-        shifted = pltpu.roll(assign, 1, 1)
-        before = jnp.where(lane == 0, pltpu.roll(shifted, 1, 0), shifted)
-        starts = (assign != before) | ((row == 0) & (lane == 0))
-        starts_f = jnp.where(starts, 1.0, 0.0)
-        upper = jnp.where(iota((LANES, LANES), 0) <= iota((LANES, LANES), 1), 1.0, 0.0).astype(BF16)
-        inner = jnp.dot(starts_f.astype(BF16), upper, preferred_element_type=F32)
-        row_total = jnp.broadcast_to(inner[:, LANES - 1 :], inner.shape).astype(BF16)
-        lower = jnp.where(iota((total_rows, total_rows), 1) < iota((total_rows, total_rows), 0), 1.0, 0.0)
-        rank = inner + jnp.dot(lower.astype(BF16), row_total, preferred_element_type=F32) - 1.0
-        rounds = (rank[total_rows - 1 :, LANES - 1 :].astype(jnp.int32) + SLOTS) // SLOTS
-        rank = rank - first
-        slot = iota((SLOTS, LANES), 0).astype(F32)
-        named = jnp.where(starts, assign, 0).astype(F32)
-        found = jnp.zeros((SLOTS, LANES), F32)
-        for q in range(total_rows):
-            rank_ref[q // rows_per, q % rows_per : q % rows_per + 1, :] = rank[q : q + 1, :]
-            found = found + jnp.where(rank[q : q + 1, :] == slot, named[q : q + 1, :], 0.0)
-        ids = jnp.broadcast_to(jnp.sum(found, axis=1, keepdims=True).astype(jnp.int32), (SLOTS, LANES))
-        id_ref[...] = ids
-        own = lax.axis_index("dp") * 16
-        pick = iota((16, LANES), 1) == iota((16, LANES), 0) + own
-        def picked(values):
-            return jnp.broadcast_to(jnp.sum(jnp.where(pick, values, 0.0), axis=1, keepdims=True), (16, LANES))
-        count = counts_ref[...]
-        fields_ref[pl.ds(14, 16, stride=FIELDS), :] = picked(label_ref[...].astype(F32))
-        fields_ref[pl.ds(14 + 16 * FIELDS, 16, stride=FIELDS), :] = picked((count // 256).astype(F32))
-        fields_ref[pl.ds(15, 16, stride=FIELDS), :] = picked((count % 256).astype(F32))
-        fields_ref[pl.ds(15 + 16 * FIELDS, 16, stride=FIELDS), :] = jnp.broadcast_to(rounds.astype(F32), (16, LANES))
-        fields_ref[pl.ds(12, SLOTS, stride=FIELDS), :] = (ids // LANES).astype(F32)
-        fields_ref[pl.ds(13, SLOTS, stride=FIELDS), :] = (ids % LANES).astype(F32)
-        acc_ref[...] = jnp.zeros_like(acc_ref)
-
+    blocks = points_ref.shape[0] // BLOCK
+    copies = [
+        pltpu.make_async_copy(
+            points_ref.at[pl.ds(n * BLOCK, BLOCK)], held_ref.at[pl.ds(n * BLOCK, BLOCK)], arrived.at[n]
+        )
+        for n in range(blocks)
+    ]
+    for copy in copies:
+        copy.start()
+
+    assign = assign_ref[...]
+    row, lane = iota(assign.shape, 0), iota(assign.shape, 1)
+    shifted = pltpu.roll(assign, 1, 1)
+    before = jnp.where(lane == 0, pltpu.roll(shifted, 1, 0), shifted)
+    starts = (assign != before) | ((row == 0) & (lane == 0))
+    upper = jnp.where(iota((LANES, LANES), 0) <= iota((LANES, LANES), 1), 1.0, 0.0).astype(BF16)
+    inner = jnp.dot(jnp.where(starts, 1.0, 0.0).astype(BF16), upper, preferred_element_type=F32)
+    row_total = jnp.broadcast_to(inner[:, LANES - 1 :], inner.shape).astype(BF16)
+    lower = jnp.where(iota((total_rows, total_rows), 1) < iota((total_rows, total_rows), 0), 1.0, 0.0)
+    rank = inner + jnp.dot(lower.astype(BF16), row_total, preferred_element_type=F32) - 1.0
+    rounds = (rank[total_rows - 1 :, LANES - 1 :].astype(jnp.int32) + SLOTS) // SLOTS
+    rank = rank - first
     slot = iota((SLOTS, LANES), 0).astype(F32)
-    ranks = rank_ref[step]
-    one_hot = jnp.concatenate(
-        [jnp.where(ranks[q : q + 1, :] == slot, 1.0, 0.0).astype(BF16) for q in range(rows_per)], axis=1
-    )
-    acc_ref[...] += jnp.dot(one_hot, points_ref[...], preferred_element_type=F32)
-
-    @pl.when(step == steps - 1)
-    def _():
-        for f in range(COLS):
-            fields_ref[pl.ds(f, SLOTS, stride=FIELDS), :] = acc_ref[:, f * LANES : (f + 1) * LANES]
-        for q in range(4):
-            turned_ref[pl.ds(q, LANES, stride=4), :] = fields_ref[q * LANES : (q + 1) * LANES, :].T
-        out_ref[...] = turned_ref[...].astype(BF16).reshape(LANES, 4, LANES)
+    named = jnp.where(starts, assign, 0).astype(F32)
+    found = jnp.zeros((SLOTS, LANES), F32)
+    for q in range(total_rows):
+        found = found + jnp.where(rank[q : q + 1, :] == slot, named[q : q + 1, :], 0.0)
+    ids = jnp.broadcast_to(jnp.sum(found, axis=1, keepdims=True).astype(jnp.int32), (SLOTS, LANES))
+    own = lax.axis_index("dp") * 16
+    pick = iota((16, LANES), 1) == iota((16, LANES), 0) + own
+
+    def picked(values):
+        return jnp.broadcast_to(jnp.sum(jnp.where(pick, values, 0.0), axis=1, keepdims=True), (16, LANES))
+
+    count = counts_ref[...]
+    fields_ref[pl.ds(14, 16, stride=FIELDS), :] = picked(label_ref[...].astype(F32))
+    fields_ref[pl.ds(14 + 16 * FIELDS, 16, stride=FIELDS), :] = picked((count // 256).astype(F32))
+    fields_ref[pl.ds(15, 16, stride=FIELDS), :] = picked((count % 256).astype(F32))
+    fields_ref[pl.ds(15 + 16 * FIELDS, 16, stride=FIELDS), :] = jnp.broadcast_to(rounds.astype(F32), (16, LANES))
+    fields_ref[pl.ds(12, SLOTS, stride=FIELDS), :] = (ids // LANES).astype(F32)
+    fields_ref[pl.ds(13, SLOTS, stride=FIELDS), :] = (ids % LANES).astype(F32)
+
+    acc = None
+    for n in range(blocks):
+        copies[n].wait()
+        rows = range(n * BLOCK // LANES, (n + 1) * BLOCK // LANES)
+        one_hot = jnp.concatenate(
+            [jnp.where(rank[q : q + 1, :] == slot, 1.0, 0.0).astype(BF16) for q in rows], axis=1
+        )
+        part = jnp.dot(one_hot, held_ref[n * BLOCK : (n + 1) * BLOCK, :], preferred_element_type=F32)
+        acc = part if acc is None else acc + part
+    for f in range(COLS):
+        fields_ref[pl.ds(f, SLOTS, stride=FIELDS), :] = acc[:, f * LANES : (f + 1) * LANES]
+    for q in range(4):
+        turned_ref[pl.ds(q, LANES, stride=4), :] = fields_ref[q * LANES : (q + 1) * LANES, :].T
+    out_ref[...] = turned_ref[...].astype(BF16).reshape(LANES, 4, LANES)
 
 
 def run_sums(points, assign, counts, labels, first_slot):
     rows, width = points.shape
-    whole = lambda shape: pl.BlockSpec(shape, lambda i: (0,) * len(shape))
+    vmem = pl.BlockSpec(memory_space=pltpu.VMEM)
     static = isinstance(first_slot, int)
-    specs = [
-        whole((rows // LANES, LANES)),
-        whole((1, LANES)),
-        whole((1, LANES)),
-        pl.BlockSpec((BLOCK, width), lambda i: (i, 0)),
-    ]
+    specs = [vmem, vmem, vmem, pl.BlockSpec(memory_space=pl.ANY)]
     args = [assign, counts, labels, points]
     if not static:
         specs = [pl.BlockSpec(memory_space=pltpu.SMEM)] + specs
@@ -107,21 +104,19 @@
 
     return pl.pallas_call(
         kernel,
-        grid=(rows // BLOCK,),
         in_specs=specs,
-        out_specs=whole((LANES, 4, LANES)),
+        out_specs=vmem,
         out_shape=jax.ShapeDtypeStruct((LANES, 4, LANES), BF16),
         scratch_shapes=[
-            pltpu.VMEM((rows // BLOCK, BLOCK // LANES, LANES), F32),
-            pltpu.VMEM((SLOTS, width), F32),
-            pltpu.VMEM((SLOTS, LANES), jnp.int32),
+            pltpu.VMEM((rows, width), BF16),
             pltpu.VMEM((SLOTS * FIELDS, LANES), F32),
             pltpu.VMEM((SLOTS * FIELDS, LANES), F32),
+            pltpu.SemaphoreType.DMA((rows // BLOCK,)),
         ],
         cost_estimate=pl.CostEstimate(
             flops=2 * 256 * rows * width, bytes_accessed=rows * width * 2, transcendentals=0
         ),
-        compiler_params=pltpu.CompilerParams(vmem_limit_bytes=12 << 20),
+        compiler_params=pltpu.CompilerParams(vmem_limit_bytes=20 << 20),
         name="run_sums",
     )(*args)
 
@@ -281,10 +276,12 @@
     assign = assign.reshape(-1, LANES)
     counts = counts.reshape(1, LANES)
     labels = l2_assign.reshape(1, LANES)
-    near = jnp.concatenate([level2] + [swapped(level2, mask) for mask in (1, 2, 3)], axis=0)
-    sums = run_sums(points, assign, counts, labels, 0)
-    centres = [near] + [swapped(near, mask) for mask in (4, 8, 12)]
-    send, acc, rounds = means(exchange(sums))
+    near = jnp.concatenate([level2, swapped(level2, 2)], axis=0)
+    sums, near = lax.optimization_barrier((run_sums(points, assign, counts, labels, 0), near))
+    centres = jnp.concatenate([near] + [swapped(near, mask) for mask in (4, 8, 12)], axis=0)
+    runs, centres = lax.optimization_barrier((exchange(sums), centres))
+    centres = [centres, swapped(centres, 1)]
+    send, acc, rounds = means(runs)
 
     def more(state):
         index, _, acc = state

time: 60.9 us -> 57.1 us (0.938)
  Pallas kernels: 13.5 us -> 10.7 us
  waiting for transfers between devices: 23 us -> 22.3 us
    ppermute x6 -> x5, waiting for transfers between devices: 13.1 us -> 1.36 us  [swapped(): return lax.ppermute(value, 'cent', [(i, i ^ mask) for i in range(16)])]
    all_to_all x2, waiting for transfers between devices: 9.91 us -> 21 us  [exchange(): return lax.all_to_all(value, BOTH, 0, 0, tiled=True)]
    pallas_call x1, Pallas kernels: 9.34 us -> 6.64 us  [run_sums(): pl.pallas_call(kernel, in_specs=specs, out_specs=vmem, out_shape=jax.Shap...]
    all_to_all x2, starting transfers between devices: 14.1 us -> 13.2 us  [exchange(): return lax.all_to_all(value, BOTH, 0, 0, tiled=True)]
    ppermute x6 -> x5, starting transfers between devices: 8.69 us -> 9.05 us  [swapped(): return lax.ppermute(value, 'cent', [(i, i ^ mask) for i in range(16)])]
  transfers between devices with their start and end apart: 8 -> 7, of which waited for: 3 -> 3; matrix products, arithmetic and copies ran while one was open for 0% -> 0% of each run, Pallas kernels for 20% -> 12%
where the time goes in v2:
time: 57.1 us; the launch traced here: 56.8 us
  waiting for transfers between devices  22.3 us (39%)
  starting transfers between devices  22.2 us (39%)
  Pallas kernels  10.7 us (19%)
  between operations  0.79 us (1%)
  loops' own time  0.65 us (1%)
    all_to_all x2, waiting for transfers between devices, exchange(): return lax.all_to_all(value, BOTH, 0, 0, tiled=True)  21 us
    all_to_all x2, starting transfers between devices, exchange(): return lax.all_to_all(value, BOTH, 0, 0, tiled=True)  13.2 us
    ppermute x5, starting transfers between devices, swapped(): return lax.ppermute(value, 'cent', [(i, i ^ mask) for i in range(16)])  9.05 us
    pallas_call x1, Pallas kernels, run_sums(): pl.pallas_call(kernel, in_specs=specs, out_specs=vmem, out_shape=jax.Shap...  6.64 us
    pallas_call x1, Pallas kernels, means(): pl.pallas_call(kernel, in_specs=[vmem] * len(args), out_specs=[vmem, vmem...  2.59 us
    pallas_call x1, Pallas kernels, finish(): pl.pallas_call(kernel, in_specs=[vmem] * (1 + len(centres)), out_specs=[v...  1.52 us
    ppermute x5, waiting for transfers between devices, swapped(): return lax.ppermute(value, 'cent', [(i, i ^ mask) for i in range(16)])  1.36 us
  transfers between devices with their start and end apart: 7, of which 3 were waited for; matrix products, arithmetic and copies ran while one was open for 0% of the time, Pallas kernels for 12%

profile of v2, /device:TPU:1, one launch (start us, length us, event | category | flops | bytes accessed | tf_op | source)
XLA Modules:
  0.0 56.8 jit_solution(6435887541684529011)
XLA Ops:
  0.6 0.0 copy-start.1
  0.6 0.0 copy-start
  0.7 0.0 copy-start.2
  0.7 0.0 copy-start.3
  0.7 3.8 %collective-permute-start = (bf16[16,1536]{1,0:T(8,128)(2,1)}, bf16[16,1536]{1,0:T(8,128)(2,1)S(1)}, u32[]{:S(2)}, u32[]{:S(2)}) collective-permute-start(bf16[16,1536]{1,0:T(8,128)(2,1)} %param.10), channel_id=1, source_target_pairs={{0,2},{1,3},{2,0},{3,1},{4,6},{5,7},{6,4},{7,5},{8,10},{9,11},{10,... | collective-permute-start | bytes 147464 | tf_op jit(solution)/shard_map/ppermute | solution.py:272
  4.5 6.6 %run_sums.2 = bf16[128,4,128]{2,1,0:T(4,128)(2,1)} custom-call(s32[32,128]{1,0:T(8,128)} %bitcast.9, s32[1,128]{1,0:T(1,128)} %bitcast.11, s32[1,128]{1,0:T(1,128)} %bitcast.13, bf16[4096,1536]{1,0:T(8,128)(2,1)} %refs_3_.1), custom_call_target="tpu_custom_call" | custom-call | flops 3221225472 | bytes 12582912 | tf_op jit(solution)/shard_map/run_sums/pallas_call | solution.py:105
  11.1 0.0 collective-permute-done
  11.1 0.0 copy-done.1
  11.2 1.3 %collective-permute-start.1 = (bf16[32,1536]{1,0:T(8,128)(2,1)S(1)}, bf16[32,1536]{1,0:T(8,128)(2,1)S(1)}, u32[]{:S(2)}, u32[]{:S(2)}) collective-permute-start(bf16[32,1536]{1,0:T(8,128)(2,1)S(1)} %pad_maximum_fusion.1), channel_id=1, source_target_pairs={{0,4},{1,5},{2,6},{3,7},{4,0},{5,1},{6,2},{7,3},{8,12},{9,13},{10,... | collective-permute-start | bytes 294920 | tf_op jit(solution)/shard_map/ppermute | solution.py:272
  12.5 2.5 %collective-permute-start.2 = (bf16[32,1536]{1,0:T(8,128)(2,1)S(1)}, bf16[32,1536]{1,0:T(8,128)(2,1)S(1)}, u32[]{:S(2)}, u32[]{:S(2)}) collective-permute-start(bf16[32,1536]{1,0:T(8,128)(2,1)S(1)} %pad_maximum_fusion.1), channel_id=1, source_target_pairs={{0,8},{1,9},{2,10},{3,11},{4,12},{5,13},{6,14},{7,15},{8,0},{9,1},... | collective-permute-start | bytes 294920 | tf_op jit(solution)/shard_map/ppermute | solution.py:272
  14.9 0.2 collective-permute-start.3
  15.1 9.4 %all-to-all-start.1 = ((bf16[128,4,128]{2,1,0:T(4,128)(2,1)}), bf16[128,4,128]{2,1,0:T(4,128)(2,1)S(1)}, u32[]{:S(2)}, u32[]{:S(2)}) async-start(bf16[128,4,128]{2,1,0:T(4,128)(2,1)} %run_sums.2), calls=%async_computation.1 | async-start | bytes 262144 | tf_op jit(solution)/shard_map/all_to_all | solution.py:268
  24.5 0.0 collective-permute-done.1
  24.5 0.0 collective-permute-done.2
  24.5 0.0 collective-permute-done.3
  24.6 9.9 %all-to-all-done.1.refs_0_ = bf16[128,4,128]{2,1,0:T(4,128)(2,1)S(1)} async-done(((bf16[128,4,128]{2,1,0:T(4,128)(2,1)}), bf16[128,4,128]{2,1,0:T(4,128)(2,1)S(1)}, u32[]{:S(2)}, u32[]{:S(2)}) %all-to-all-start.1) | async-done | bytes 131104 | tf_op jit(solution)/shard_map/all_to_all | solution.py:268
  34.4 2.6 %means.2 = (bf16[128,16,128]{2,1,0:T(8,128)(2,1)}, f32[256,128]{1,0:T(8,128)S(1)}, s32[1]{0:T(128)}) custom-call(bf16[128,4,128]{2,1,0:T(4,128)(2,1)S(1)} %all-to-all-done.1.refs_0_), custom_call_target="tpu_custom_call" | custom-call | tf_op jit(solution)/shard_map/means/pallas_call | solution.py:198
  37.0 0.0 copy-done
  37.0 0.0 copy-done.2
  37.1 0.0 copy-done.3
  37.1 0.7 %while.12 = (s32[]{:T(128)}, bf16[128,16,128]{2,1,0:T(8,128)(2,1)}, f32[256,128]{1,0:T(8,128)S(1)}, s32[1]{0:T(128)}, s32[32,128]{1,0:T(8,128)S(1)}, /*index=5*/...) while((s32[]{:T(128)}, bf16[128,16,128]{2,1,0:T(8,128)(2,1)}, ...), condition=%wide.region_1.0_spmd, body=%wide.region_0.0_spmd.sunk | while | flops 3221225472 | bytes 13238417 | solution.py:292
  37.7 3.8 %all-to-all-start.2 = ((bf16[128,16,128]{2,1,0:T(8,128)(2,1)}), bf16[128,16,128]{2,1,0:T(8,128)(2,1)S(1)}, u32[]{:S(2)}, u32[]{:S(2)}) async-start(bf16[128,16,128]{2,1,0:T(8,128)(2,1)} %get-tuple-element.63), calls=%async_computation.2 | async-start | bytes 1048576 | tf_op jit(solution)/shard_map/all_to_all | solution.py:268
  41.6 1.3 %collective-permute-start.4 = (bf16[128,1536]{1,0:T(8,128)(2,1)S(1)}, bf16[128,1536]{1,0:T(8,128)(2,1)S(1)}, u32[]{:S(2)}, u32[]{:S(2)}) collective-permute-start(bf16[128,1536]{1,0:T(8,128)(2,1)S(1)} %pad_maximum_fusion.refs_1_), channel_id=1, source_target_pairs={{0,1},{1,0},{2,3},{3,2},{4,5},{5,4},{6,7},{7,6},{8,9},{9,8},{10,11... | collective-permute-start | bytes 1179656 | tf_op jit(solution)/shard_map/ppermute | solution.py:272
  42.8 1.3 %collective-permute-done.4.refs_2_ = bf16[128,1536]{1,0:T(8,128)(2,1)S(1)} collective-permute-done((bf16[128,1536]{1,0:T(8,128)(2,1)S(1)}, bf16[128,1536]{1,0:T(8,128)(2,1)S(1)}, u32[]{:S(2)}, u32[]{:S(2)}) %collective-permute-start.4) | collective-permute-done | bytes 393248 | tf_op jit(solution)/shard_map/ppermute | solution.py:272
  44.2 11.1 %all-to-all-done.2.refs_0_ = bf16[128,16,128]{2,1,0:T(8,128)(2,1)S(1)} async-done(((bf16[128,16,128]{2,1,0:T(8,128)(2,1)}), bf16[128,16,128]{2,1,0:T(8,128)(2,1)S(1)}, u32[]{:S(2)}, u32[]{:S(2)}) %all-to-all-start.2) | async-done | bytes 524320 | tf_op jit(solution)/shard_map/all_to_all | solution.py:268
  55.3 1.5 %finish.1 = (bf16[128,1536]{1,0:T(8,128)(2,1)}, f32[1,128]{1,0:T(1,128)}, bf16[16,1536]{1,0:T(8,128)(2,1)}) custom-call(bf16[128,16,128]{2,1,0:T(8,128)(2,1)S(1)} %all-to-all-done.2.refs_0_, bf16[128,1536]{1,0:T(8,128)(2,1)S(1)} %pad_maximum_fusion.refs_1_, bf16[128,1536]{1,0:T(8,128)(2,1)S(1)} %collective-permute-done.4.refs_2_), custom_call_target="tpu_custom_call" | custom-call | tf_op jit(solution)/shard_map/finish/pallas_call | solution.py:252
  (2 shorter events, 0.0 us)
Async XLA Ops:
  0.6 10.5 %copy-start.1 = (bf16[16,1536]{1,0:T(8,128)(2,1)S(1)}, bf16[16,1536]{1,0:T(8,128)(2,1)}, u32[]{:S(2)}) copy-start(bf16[16,1536]{1,0:T(8,128)(2,1)} %param.10) | copy-start | bytes 147460
  0.6 36.4 %copy-start = (s32[4096]{0:T(1024)S(1)}, s32[4096]{0:T(1024)}, u32[]{:S(2)}) copy-start(s32[4096]{0:T(1024)} %param.8) | copy-start | bytes 49156
  0.7 36.4 %copy-start.2 = (s32[128]{0:T(128)S(1)}, s32[128]{0:T(128)}, u32[]{:S(2)}) copy-start(s32[128]{0:T(128)} %param.9) | copy-start | bytes 1540
  0.7 36.4 %copy-start.3 = (s32[128,1]{0,1:T(1,128)S(1)}, s32[128,1]{0,1:T(1,128)}, u32[]{:S(2)}) copy-start(s32[128,1]{0,1:T(1,128)} %param.11) | copy-start | bytes 1540
  0.7 10.5 %collective-permute-start = (bf16[16,1536]{1,0:T(8,128)(2,1)}, bf16[16,1536]{1,0:T(8,128)(2,1)S(1)}, u32[]{:S(2)}, u32[]{:S(2)}) collective-permute-start(bf16[16,1536]{1,0:T(8,128)(2,1)} %param.10), channel_id=1, source_target_pairs={{0,2},{1,3},{2,0},{3,1},{4,6},{5,7},{6,4},{7,5},{8,10},{9,11},{10,... | collective-permute-start | bytes 147464 | tf_op jit(solution)/shard_map/ppermute | solution.py:272
  11.2 13.3 %collective-permute-start.1 = (bf16[32,1536]{1,0:T(8,128)(2,1)S(1)}, bf16[32,1536]{1,0:T(8,128)(2,1)S(1)}, u32[]{:S(2)}, u32[]{:S(2)}) collective-permute-start(bf16[32,1536]{1,0:T(8,128)(2,1)S(1)} %pad_maximum_fusion.1), channel_id=1, source_target_pairs={{0,4},{1,5},{2,6},{3,7},{4,0},{5,1},{6,2},{7,3},{8,12},{9,13},{10,... | collective-permute-start | bytes 294920 | tf_op jit(solution)/shard_map/ppermute | solution.py:272
  12.5 12.1 %collective-permute-start.2 = (bf16[32,1536]{1,0:T(8,128)(2,1)S(1)}, bf16[32,1536]{1,0:T(8,128)(2,1)S(1)}, u32[]{:S(2)}, u32[]{:S(2)}) collective-permute-start(bf16[32,1536]{1,0:T(8,128)(2,1)S(1)} %pad_maximum_fusion.1), channel_id=1, source_target_pairs={{0,8},{1,9},{2,10},{3,11},{4,12},{5,13},{6,14},{7,15},{8,0},{9,1},... | collective-permute-start | bytes 294920 | tf_op jit(solution)/shard_map/ppermute | solution.py:272
  14.9 9.6 %collective-permute-start.3 = (bf16[32,1536]{1,0:T(8,128)(2,1)S(1)}, bf16[32,1536]{1,0:T(8,128)(2,1)S(1)}, u32[]{:S(2)}, u32[]{:S(2)}) collective-permute-start(bf16[32,1536]{1,0:T(8,128)(2,1)S(1)} %pad_maximum_fusion.1), channel_id=1, source_target_pairs={{0,12},{1,13},{2,14},{3,15},{4,8},{5,9},{6,10},{7,11},{8,4},{9,5},... | collective-permute-start | bytes 294920 | tf_op jit(solution)/shard_map/ppermute | solution.py:272
  15.1 19.3 %all-to-all-start.1 = ((bf16[128,4,128]{2,1,0:T(4,128)(2,1)}), bf16[128,4,128]{2,1,0:T(4,128)(2,1)S(1)}, u32[]{:S(2)}, u32[]{:S(2)}) async-start(bf16[128,4,128]{2,1,0:T(4,128)(2,1)} %run_sums.2), calls=%async_computation.1 | async-start | bytes 262144 | tf_op jit(solution)/shard_map/all_to_all | solution.py:268
  37.7 17.6 %all-to-all-start.2 = ((bf16[128,16,128]{2,1,0:T(8,128)(2,1)}), bf16[128,16,128]{2,1,0:T(8,128)(2,1)S(1)}, u32[]{:S(2)}, u32[]{:S(2)}) async-start(bf16[128,16,128]{2,1,0:T(8,128)(2,1)} %get-tuple-element.63), calls=%async_computation.2 | async-start | bytes 1048576 | tf_op jit(solution)/shard_map/all_to_all | solution.py:268
  41.6 2.6 %collective-permute-start.4 = (bf16[128,1536]{1,0:T(8,128)(2,1)S(1)}, bf16[128,1536]{1,0:T(8,128)(2,1)S(1)}, u32[]{:S(2)}, u32[]{:S(2)}) collective-permute-start(bf16[128,1536]{1,0:T(8,128)(2,1)S(1)} %pad_maximum_fusion.refs_1_), channel_id=1, source_target_pairs={{0,1},{1,0},{2,3},{3,2},{4,5},{5,4},{6,7},{7,6},{8,9},{9,8},{10,11... | collective-permute-start | bytes 1179656 | tf_op jit(solution)/shard_map/ppermute | solution.py:272

commit v3 on v2

--- a/solution.py
+++ b/solution.py
@@ -29,8 +29,8 @@
         first = slot_ref[0].astype(F32)
     else:
         first = float(first_slot)
-    assign_ref, counts_ref, label_ref, points_ref, out_ref, held_ref, fields_ref, turned_ref, arrived = refs
-    total_rows = assign_ref.shape[0]
+    assign_hbm, counts_hbm, label_hbm, points_ref, out_ref, assign_ref, counts_ref, label_ref, held_ref, fields_ref, turned_ref, arrived, small = refs
+    total_rows = assign_hbm.shape[0]
     blocks = points_ref.shape[0] // BLOCK
     copies = [
         pltpu.make_async_copy(
@@ -38,8 +38,18 @@
         )
         for n in range(blocks)
     ]
+    numbers = [
+        pltpu.make_async_copy(source, target, small.at[n])
+        for n, (source, target) in enumerate(
+            ((assign_hbm, assign_ref), (counts_hbm, counts_ref), (label_hbm, label_ref))
+        )
+    ]
+    for copy in numbers:
+        copy.start()
     for copy in copies:
-        copy.start()
+        copy.start(priority=1)
+    for copy in numbers:
+        copy.wait()
 
     assign = assign_ref[...]
     row, lane = iota(assign.shape, 0), iota(assign.shape, 1)
@@ -93,7 +103,7 @@
     rows, width = points.shape
     vmem = pl.BlockSpec(memory_space=pltpu.VMEM)
     static = isinstance(first_slot, int)
-    specs = [vmem, vmem, vmem, pl.BlockSpec(memory_space=pl.ANY)]
+    specs = [pl.BlockSpec(memory_space=pl.ANY)] * 4
     args = [assign, counts, labels, points]
     if not static:
         specs = [pl.BlockSpec(memory_space=pltpu.SMEM)] + specs
@@ -108,10 +118,14 @@
         out_specs=vmem,
         out_shape=jax.ShapeDtypeStruct((LANES, 4, LANES), BF16),
         scratch_shapes=[
+            pltpu.VMEM(assign.shape, jnp.int32),
+            pltpu.VMEM(counts.shape, jnp.int32),
+            pltpu.VMEM(labels.shape, jnp.int32),
             pltpu.VMEM((rows, width), BF16),
             pltpu.VMEM((SLOTS * FIELDS, LANES), F32),
             pltpu.VMEM((SLOTS * FIELDS, LANES), F32),
             pltpu.SemaphoreType.DMA((rows // BLOCK,)),
+            pltpu.SemaphoreType.DMA((3,)),
         ],
         cost_estimate=pl.CostEstimate(
             flops=2 * 256 * rows * width, bytes_accessed=rows * width * 2, transcendentals=0
@@ -276,12 +290,13 @@
     assign = assign.reshape(-1, LANES)
     counts = counts.reshape(1, LANES)
     labels = l2_assign.reshape(1, LANES)
+    sums, level2 = lax.optimization_barrier((run_sums(points, assign, counts, labels, 0), level2))
     near = jnp.concatenate([level2, swapped(level2, 2)], axis=0)
-    sums, near = lax.optimization_barrier((run_sums(points, assign, counts, labels, 0), near))
+    runs = exchange(sums)
     centres = jnp.concatenate([near] + [swapped(near, mask) for mask in (4, 8, 12)], axis=0)
-    runs, centres = lax.optimization_barrier((exchange(sums), centres))
+    send, acc, rounds = means(runs)
+    send, centres = lax.optimization_barrier((send, centres))
     centres = [centres, swapped(centres, 1)]
-    send, acc, rounds = means(runs)
 
     def more(state):
         index, _, acc = state

time: 57.1 us -> 53.6 us (0.939)
  waiting for transfers between devices: 22.3 us -> 18.5 us
  starting transfers between devices: 22.2 us -> 23.4 us
  Pallas kernels: 10.7 us -> 9.94 us
    all_to_all x2, waiting for transfers between devices: 21 us -> 17.1 us  [exchange(): return lax.all_to_all(value, BOTH, 0, 0, tiled=True)]
    all_to_all x2, starting transfers between devices: 13.2 us -> 14.6 us  [exchange(): return lax.all_to_all(value, BOTH, 0, 0, tiled=True)]
    pallas_call x1, Pallas kernels: 6.64 us -> 5.85 us  [run_sums(): pl.pallas_call(kernel, in_specs=specs, out_specs=vmem, out_shape=jax.Shap...]
  transfers between devices with their start and end apart: 7 -> 7, of which waited for: 3 -> 3; matrix products, arithmetic and copies ran while one was open for 0% -> 0% of each run, Pallas kernels for 12% -> 5%
where the time goes in v3:
time: 53.6 us; the launch traced here: 53.4 us
  starting transfers between devices  23.4 us (44%)
  waiting for transfers between devices  18.5 us (35%)
  Pallas kernels  9.94 us (19%)
  between operations  0.8 us (1%)
  loops' own time  0.65 us (1%)
    all_to_all x2, waiting for transfers between devices, exchange(): return lax.all_to_all(value, BOTH, 0, 0, tiled=True)  17.1 us
    all_to_all x2, starting transfers between devices, exchange(): return lax.all_to_all(value, BOTH, 0, 0, tiled=True)  14.6 us
    ppermute x5, starting transfers between devices, swapped(): return lax.ppermute(value, 'cent', [(i, i ^ mask) for i in range(16)])  8.83 us
    pallas_call x1, Pallas kernels, run_sums(): pl.pallas_call(kernel, in_specs=specs, out_specs=vmem, out_shape=jax.Shap...  5.85 us
    pallas_call x1, Pallas kernels, means(): pl.pallas_call(kernel, in_specs=[vmem] * len(args), out_specs=[vmem, vmem...  2.57 us
    pallas_call x1, Pallas kernels, finish(): pl.pallas_call(kernel, in_specs=[vmem] * (1 + len(centres)), out_specs=[v...  1.52 us
    ppermute x5, waiting for transfers between devices, swapped(): return lax.ppermute(value, 'cent', [(i, i ^ mask) for i in range(16)])  1.36 us
  transfers between devices with their start and end apart: 7, of which 3 were waited for; matrix products, arithmetic and copies ran while one was open for 0% of the time, Pallas kernels for 5%

profile of v3, /device:TPU:1, one launch (start us, length us, event | category | flops | bytes accessed | tf_op | source)
XLA Modules:
  0.0 53.4 jit_solution(8614644249367397363)
XLA Ops:
  0.6 0.0 copy-start.3
  0.6 0.0 copy-start.2
  0.7 0.0 copy-start
  0.7 0.0 copy-start.1
  0.7 5.9 %run_sums.2 = bf16[128,4,128]{2,1,0:T(4,128)(2,1)} custom-call(s32[32,128]{1,0:T(8,128)} %bitcast.9, s32[1,128]{1,0:T(1,128)} %bitcast.11, s32[1,128]{1,0:T(1,128)} %bitcast.13, bf16[4096,1536]{1,0:T(8,128)(2,1)} %refs_3_.1), custom_call_target="tpu_custom_call" | custom-call | flops 3221225472 | bytes 12582912 | tf_op jit(solution)/shard_map/run_sums/pallas_call | solution.py:115
  6.5 0.0 copy-done.1
  6.5 3.8 %collective-permute-start = (bf16[16,1536]{1,0:T(8,128)(2,1)S(1)}, bf16[16,1536]{1,0:T(8,128)(2,1)S(1)}, u32[]{:S(2)}, u32[]{:S(2)}) collective-permute-start(bf16[16,1536]{1,0:T(8,128)(2,1)S(1)} %copy-done.1), channel_id=1, source_target_pairs={{0,2},{1,3},{2,0},{3,1},{4,6},{5,7},{6,4},{7,5},{8,10},{9,11},{10,... | collective-permute-start | bytes 147464 | tf_op jit(solution)/shard_map/ppermute | solution.py:286
  10.4 8.8 %all-to-all-start.1 = ((bf16[128,4,128]{2,1,0:T(4,128)(2,1)}), bf16[128,4,128]{2,1,0:T(4,128)(2,1)S(1)}, u32[]{:S(2)}, u32[]{:S(2)}) async-start(bf16[128,4,128]{2,1,0:T(4,128)(2,1)} %run_sums.2), calls=%async_computation.1 | async-start | bytes 262144 | tf_op jit(solution)/shard_map/all_to_all | solution.py:282
  19.2 0.0 collective-permute-done
  19.2 1.5 %collective-permute-start.1 = (bf16[32,1536]{1,0:T(8,128)(2,1)S(1)}, bf16[32,1536]{1,0:T(8,128)(2,1)S(1)}, u32[]{:S(2)}, u32[]{:S(2)}) collective-permute-start(bf16[32,1536]{1,0:T(8,128)(2,1)S(1)} %get-tuple-element.84), channel_id=1, source_target_pairs={{0,4},{1,5},{2,6},{3,7},{4,0},{5,1},{6,2},{7,3},{8,12},{9,13},{10,... | collective-permute-start | bytes 294920 | tf_op jit(solution)/shard_map/ppermute | solution.py:286
  20.7 1.8 %collective-permute-start.3 = (bf16[32,1536]{1,0:T(8,128)(2,1)S(1)}, bf16[32,1536]{1,0:T(8,128)(2,1)S(1)}, u32[]{:S(2)}, u32[]{:S(2)}) collective-permute-start(bf16[32,1536]{1,0:T(8,128)(2,1)S(1)} %get-tuple-element.84), channel_id=1, source_target_pairs={{0,12},{1,13},{2,14},{3,15},{4,8},{5,9},{6,10},{7,11},{8,4},{9,5},... | collective-permute-start | bytes 294920 | tf_op jit(solution)/shard_map/ppermute | solution.py:286
  22.5 0.6 %collective-permute-start.2 = (bf16[32,1536]{1,0:T(8,128)(2,1)S(1)}, bf16[32,1536]{1,0:T(8,128)(2,1)S(1)}, u32[]{:S(2)}, u32[]{:S(2)}) collective-permute-start(bf16[32,1536]{1,0:T(8,128)(2,1)S(1)} %get-tuple-element.84), channel_id=1, source_target_pairs={{0,8},{1,9},{2,10},{3,11},{4,12},{5,13},{6,14},{7,15},{8,0},{9,1},... | collective-permute-start | bytes 294920 | tf_op jit(solution)/shard_map/ppermute | solution.py:286
  23.1 6.0 %all-to-all-done.1.refs_0_ = bf16[128,4,128]{2,1,0:T(4,128)(2,1)S(1)} async-done(((bf16[128,4,128]{2,1,0:T(4,128)(2,1)}), bf16[128,4,128]{2,1,0:T(4,128)(2,1)S(1)}, u32[]{:S(2)}, u32[]{:S(2)}) %all-to-all-start.1) | async-done | bytes 131104 | tf_op jit(solution)/shard_map/all_to_all | solution.py:282
  29.1 2.6 %means.2 = (bf16[128,16,128]{2,1,0:T(8,128)(2,1)}, f32[256,128]{1,0:T(8,128)S(1)}, s32[1]{0:T(128)}) custom-call(bf16[128,4,128]{2,1,0:T(4,128)(2,1)S(1)} %all-to-all-done.1.refs_0_), custom_call_target="tpu_custom_call" | custom-call | tf_op jit(solution)/shard_map/means/pallas_call | solution.py:212
  31.7 0.0 collective-permute-done.1
  31.7 0.0 collective-permute-done.2
  31.8 0.0 collective-permute-done.3
  31.8 0.0 copy-done.3
  31.8 0.0 copy-done.2
  31.8 0.0 copy-done
  31.8 0.7 %while.12 = (s32[]{:T(128)}, bf16[128,16,128]{2,1,0:T(8,128)(2,1)}, f32[256,128]{1,0:T(8,128)S(1)}, s32[1]{0:T(128)}, s32[32,128]{1,0:T(8,128)S(1)}, /*index=5*/...) while((s32[]{:T(128)}, bf16[128,16,128]{2,1,0:T(8,128)(2,1)}, ...), condition=%wide.region_1.0_spmd, body=%wide.region_0.0_spmd.sunk | while | flops 3221225472 | bytes 13238417 | solution.py:307
  32.5 5.8 %all-to-all-start.2 = ((bf16[128,16,128]{2,1,0:T(8,128)(2,1)}), bf16[128,16,128]{2,1,0:T(8,128)(2,1)S(1)}, u32[]{:S(2)}, u32[]{:S(2)}) async-start(bf16[128,16,128]{2,1,0:T(8,128)(2,1)} %get-tuple-element.63), calls=%async_computation.2 | async-start | bytes 1048576 | tf_op jit(solution)/shard_map/all_to_all | solution.py:282
  38.3 1.1 %collective-permute-start.4 = (bf16[128,1536]{1,0:T(8,128)(2,1)S(1)}, bf16[128,1536]{1,0:T(8,128)(2,1)S(1)}, u32[]{:S(2)}, u32[]{:S(2)}) collective-permute-start(bf16[128,1536]{1,0:T(8,128)(2,1)S(1)} %constant_dynamic-update-slice_fusion.2.refs_1_), channel_id=1, source_target_pairs={{0,1},{1,0},{2,3},{3,2},{4,5},{5,4},{6,7},{7,6},{8,9},{9,8},{10,11... | collective-permute-start | bytes 1179656 | tf_op jit(solution)/shard_map/ppermute | solution.py:286
  39.4 1.3 %collective-permute-done.4.refs_2_ = bf16[128,1536]{1,0:T(8,128)(2,1)S(1)} collective-permute-done((bf16[128,1536]{1,0:T(8,128)(2,1)S(1)}, bf16[128,1536]{1,0:T(8,128)(2,1)S(1)}, u32[]{:S(2)}, u32[]{:S(2)}) %collective-permute-start.4) | collective-permute-done | bytes 393248 | tf_op jit(solution)/shard_map/ppermute | solution.py:286
  40.8 11.1 %all-to-all-done.2.refs_0_ = bf16[128,16,128]{2,1,0:T(8,128)(2,1)S(1)} async-done(((bf16[128,16,128]{2,1,0:T(8,128)(2,1)}), bf16[128,16,128]{2,1,0:T(8,128)(2,1)S(1)}, u32[]{:S(2)}, u32[]{:S(2)}) %all-to-all-start.2) | async-done | bytes 524320 | tf_op jit(solution)/shard_map/all_to_all | solution.py:282
  51.9 1.5 %finish.1 = (bf16[128,1536]{1,0:T(8,128)(2,1)}, f32[1,128]{1,0:T(1,128)}, bf16[16,1536]{1,0:T(8,128)(2,1)}) custom-call(bf16[128,16,128]{2,1,0:T(8,128)(2,1)S(1)} %all-to-all-done.2.refs_0_, bf16[128,1536]{1,0:T(8,128)(2,1)S(1)} %constant_dynamic-update-slice_fusion.2.refs_1_, bf16[128,1536]{1,0:T(8,128)(2,1)S(1)} %collective-permute-done.4.refs_2_), custom_call_target="tpu_custom_call" | custom-call | tf_op jit(solution)/shard_map/finish/pallas_call | solution.py:266
  (5 shorter events, 0.0 us)
Async XLA Ops:
  0.6 31.2 %copy-start.3 = (s32[128,1]{0,1:T(1,128)S(1)}, s32[128,1]{0,1:T(1,128)}, u32[]{:S(2)}) copy-start(s32[128,1]{0,1:T(1,128)} %param.11) | copy-start | bytes 1540
  0.6 31.2 %copy-start.2 = (s32[128]{0:T(128)S(1)}, s32[128]{0:T(128)}, u32[]{:S(2)}) copy-start(s32[128]{0:T(128)} %param.9) | copy-start | bytes 1540
  0.7 31.2 %copy-start = (s32[4096]{0:T(1024)S(1)}, s32[4096]{0:T(1024)}, u32[]{:S(2)}) copy-start(s32[4096]{0:T(1024)} %param.8) | copy-start | bytes 49156
  0.7 5.9 %copy-start.1 = (bf16[16,1536]{1,0:T(8,128)(2,1)S(1)}, bf16[16,1536]{1,0:T(8,128)(2,1)}, u32[]{:S(2)}) copy-start(bf16[16,1536]{1,0:T(8,128)(2,1)} %param.10) | copy-start | bytes 147460
  6.5 12.7 %collective-permute-start = (bf16[16,1536]{1,0:T(8,128)(2,1)S(1)}, bf16[16,1536]{1,0:T(8,128)(2,1)S(1)}, u32[]{:S(2)}, u32[]{:S(2)}) collective-permute-start(bf16[16,1536]{1,0:T(8,128)(2,1)S(1)} %copy-done.1), channel_id=1, source_target_pairs={{0,2},{1,3},{2,0},{3,1},{4,6},{5,7},{6,4},{7,5},{8,10},{9,11},{10,... | collective-permute-start | bytes 147464 | tf_op jit(solution)/shard_map/ppermute | solution.py:286
  10.4 18.7 %all-to-all-start.1 = ((bf16[128,4,128]{2,1,0:T(4,128)(2,1)}), bf16[128,4,128]{2,1,0:T(4,128)(2,1)S(1)}, u32[]{:S(2)}, u32[]{:S(2)}) async-start(bf16[128,4,128]{2,1,0:T(4,128)(2,1)} %run_sums.2), calls=%async_computation.1 | async-start | bytes 262144 | tf_op jit(solution)/shard_map/all_to_all | solution.py:282
  19.2 12.5 %collective-permute-start.1 = (bf16[32,1536]{1,0:T(8,128)(2,1)S(1)}, bf16[32,1536]{1,0:T(8,128)(2,1)S(1)}, u32[]{:S(2)}, u32[]{:S(2)}) collective-permute-start(bf16[32,1536]{1,0:T(8,128)(2,1)S(1)} %get-tuple-element.84), channel_id=1, source_target_pairs={{0,4},{1,5},{2,6},{3,7},{4,0},{5,1},{6,2},{7,3},{8,12},{9,13},{10,... | collective-permute-start | bytes 294920 | tf_op jit(solution)/shard_map/ppermute | solution.py:286
  20.7 11.1 %collective-permute-start.3 = (bf16[32,1536]{1,0:T(8,128)(2,1)S(1)}, bf16[32,1536]{1,0:T(8,128)(2,1)S(1)}, u32[]{:S(2)}, u32[]{:S(2)}) collective-permute-start(bf16[32,1536]{1,0:T(8,128)(2,1)S(1)} %get-tuple-element.84), channel_id=1, source_target_pairs={{0,12},{1,13},{2,14},{3,15},{4,8},{5,9},{6,10},{7,11},{8,4},{9,5},... | collective-permute-start | bytes 294920 | tf_op jit(solution)/shard_map/ppermute | solution.py:286
  22.5 9.3 %collective-permute-start.2 = (bf16[32,1536]{1,0:T(8,128)(2,1)S(1)}, bf16[32,1536]{1,0:T(8,128)(2,1)S(1)}, u32[]{:S(2)}, u32[]{:S(2)}) collective-permute-start(bf16[32,1536]{1,0:T(8,128)(2,1)S(1)} %get-tuple-element.84), channel_id=1, source_target_pairs={{0,8},{1,9},{2,10},{3,11},{4,12},{5,13},{6,14},{7,15},{8,0},{9,1},... | collective-permute-start | bytes 294920 | tf_op jit(solution)/shard_map/ppermute | solution.py:286
  32.5 19.4 %all-to-all-start.2 = ((bf16[128,16,128]{2,1,0:T(8,128)(2,1)}), bf16[128,16,128]{2,1,0:T(8,128)(2,1)S(1)}, u32[]{:S(2)}, u32[]{:S(2)}) async-start(bf16[128,16,128]{2,1,0:T(8,128)(2,1)} %get-tuple-element.63), calls=%async_computation.2 | async-start | bytes 1048576 | tf_op jit(solution)/shard_map/all_to_all | solution.py:282
  38.3 2.5 %collective-permute-start.4 = (bf16[128,1536]{1,0:T(8,128)(2,1)S(1)}, bf16[128,1536]{1,0:T(8,128)(2,1)S(1)}, u32[]{:S(2)}, u32[]{:S(2)}) collective-permute-start(bf16[128,1536]{1,0:T(8,128)(2,1)S(1)} %constant_dynamic-update-slice_fusion.2.refs_1_), channel_id=1, source_target_pairs={{0,1},{1,0},{2,3},{3,2},{4,5},{5,4},{6,7},{7,6},{8,9},{9,8},{10,11... | collective-permute-start | bytes 1179656 | tf_op jit(solution)/shard_map/ppermute | solution.py:286

commit v4 on v3

--- a/solution.py
+++ b/solution.py
@@ -144,18 +144,21 @@
     wide_ref[...] = runs_ref[...].reshape(4 * LANES, LANES).astype(F32)
     for q in range(4):
         field_ref[q * LANES : (q + 1) * LANES, :] = wide_ref[pl.ds(q, LANES, stride=4), :].T
-    low_id = iota((LANES, LANES), 0).astype(F32)
-    high_id = iota((16, LANES), 0).astype(F32)
+    low_ids = [(iota((16, LANES), 0) + 16 * k).astype(BF16) for k in range(8)]
+    one, zero = jnp.ones((16, LANES), BF16), jnp.zeros((16, LANES), BF16)
+
+    def spread_row(ref, row):
+        return jnp.broadcast_to(ref[row : row + 1, :], (16, LANES)).astype(BF16)
+
     acc = before_ref[...] if carried else None
     for pair in range(SLOTS // 2):
         lefts, rights = [], []
         for r in (2 * pair, 2 * pair + 1):
-            block = field_ref[r * FIELDS : (r + 1) * FIELDS, :]
-            high = jnp.where(block[12:13, :] == high_id, 1.0, 0.0)
-            rights.append(jnp.where(block[13:14, :] == low_id, 1.0, 0.0).astype(BF16))
-            lefts.append(
-                jnp.concatenate([(high[a : a + 1, :] * block).astype(BF16) for a in range(16)], axis=0)
-            )
+            block = field_ref[r * FIELDS : (r + 1) * FIELDS, :].astype(BF16)
+            high = spread_row(field_ref, r * FIELDS + 12)
+            low = spread_row(field_ref, r * FIELDS + 13)
+            lefts.append(jnp.concatenate([jnp.where(high == a, block, zero) for a in range(16)], axis=0))
+            rights.append(jnp.concatenate([jnp.where(low == ids, one, zero) for ids in low_ids], axis=0))
         part = nt_dot(jnp.concatenate(lefts, axis=1), jnp.concatenate(rights, axis=1))
         acc = part if acc is None else acc + part
     acc_ref[...] = acc
@@ -173,26 +176,27 @@
     rounds = jnp.max(field_ref[15 + 16 * FIELDS : 16 + 16 * FIELDS, :])
     rounds_ref[0] = rounds.astype(jnp.int32)
 
-    sums_two = jnp.zeros((16, COLS * 16), F32)
-    members = jnp.zeros((16, 16), F32)
+    sums_two = None
     for pair in range(8):
-        owners, insides, values = [], [], []
+        owners, values = [], []
         for a in (2 * pair, 2 * pair + 1):
-            mean = (acc[a * 16 : (a + 1) * 16, :] / count[a : a + 1, :]).astype(BF16).astype(F32)
-            send_ref[a * 16 : (a + 1) * 16, :] = mean
-            own = label[a : a + 1, :]
+            send_ref[a * 16 : (a + 1) * 16, :] = (
+                (acc[a * 16 : (a + 1) * 16, :] / count[a : a + 1, :]).astype(BF16).astype(F32)
+            )
+            own = jnp.broadcast_to(label[a : a + 1, :], (16, LANES))
             owners.append(jnp.where(own // 16 == iota((16, LANES), 0), 1.0, 0.0).astype(BF16))
-            inside = jnp.where(own % 16 == iota((16, LANES), 0), 1.0, 0.0)
-            insides.append(inside.astype(BF16))
+            inside = jnp.where(own % 16 == iota((16, LANES), 0), 1.0, 0.0).astype(BF16)
             values.append(
-                jnp.concatenate([(inside * mean[f : f + 1, :]).astype(BF16) for f in range(COLS)], axis=0)
+                jnp.concatenate(
+                    [jnp.where(inside == one, spread_row(send_ref, a * 16 + f), zero) for f in range(COLS)]
+                    + [inside],
+                    axis=0,
+                )
             )
-        left = jnp.concatenate(owners, axis=1)
-        sums_two = sums_two + nt_dot(left, jnp.concatenate(values, axis=1))
-        members = members + nt_dot(left, jnp.concatenate(insides, axis=1))
-    repeat = jnp.where(iota((16, COLS * 16), 1) % 16 == iota((16, COLS * 16), 0), 1.0, 0.0).astype(BF16)
-    members_wide = jnp.dot(members.astype(BF16), repeat, preferred_element_type=F32)
-    level2 = sums_two / members_wide
+        part = nt_dot(jnp.concatenate(values, axis=1), jnp.concatenate(owners, axis=1))
+        sums_two = part if sums_two is None else sums_two + part
+    members = sums_two[COLS * 16 :, :]
+    level2 = jnp.concatenate([sums_two[f * 16 : (f + 1) * 16, :] / members for f in range(COLS)], axis=0).T
     send_ref[pl.ds(12, 16, stride=16), :] = level2[:, :LANES]
     send_ref[pl.ds(13, 16, stride=16), :] = jnp.concatenate(
         [level2[:, LANES:], jnp.zeros((16, 2 * LANES - COLS * 16), F32)], axis=1
@@ -286,6 +290,10 @@
     return lax.ppermute(value, "cent", [(i, i ^ mask) for i in range(16)])
 
 
+def shifted(value, step):
+    return lax.ppermute(value, "cent", [(i, (i + step) % 16) for i in range(16)])
+
+
 def body(points, assign, counts, level2, l2_assign):
     assign = assign.reshape(-1, LANES)
     counts = counts.reshape(1, LANES)
@@ -295,7 +303,6 @@
     runs = exchange(sums)
     centres = jnp.concatenate([near] + [swapped(near, mask) for mask in (4, 8, 12)], axis=0)
     send, acc, rounds = means(runs)
-    send, centres = lax.optimization_barrier((send, centres))
     centres = [centres, swapped(centres, 1)]
 
     def more(state):

time: 53.6 us -> 52 us (0.970)
  starting transfers between devices: 23.4 us -> 22.1 us
    all_to_all x2, starting transfers between devices: 14.6 us -> 13.2 us  [exchange(): return lax.all_to_all(value, BOTH, 0, 0, tiled=True)]
where the time goes in v4:
time: 52 us; the launch traced here: 51.8 us
  starting transfers between devices  22.1 us (42%)
  waiting for transfers between devices  18.3 us (35%)
  Pallas kernels  9.84 us (19%)
  between operations  0.8 us (2%)
  loops' own time  0.65 us (1%)
    all_to_all x2, waiting for transfers between devices, exchange(): return lax.all_to_all(value, BOTH, 0, 0, tiled=True)  17 us
    all_to_all x2, starting transfers between devices, exchange(): return lax.all_to_all(value, BOTH, 0, 0, tiled=True)  13.2 us
    ppermute x5, starting transfers between devices, swapped(): return lax.ppermute(value, 'cent', [(i, i ^ mask) for i in range(16)])  8.92 us
    pallas_call x1, Pallas kernels, run_sums(): pl.pallas_call(kernel, in_specs=specs, out_specs=vmem, out_shape=jax.Shap...  5.85 us
    pallas_call x1, Pallas kernels, means(): pl.pallas_call(kernel, in_specs=[vmem] * len(args), out_specs=[vmem, vmem...  2.47 us
    pallas_call x1, Pallas kernels, finish(): pl.pallas_call(kernel, in_specs=[vmem] * (1 + len(centres)), out_specs=[v...  1.52 us
    ppermute x5, waiting for transfers between devices, swapped(): return lax.ppermute(value, 'cent', [(i, i ^ mask) for i in range(16)])  1.36 us
  transfers between devices with their start and end apart: 7, of which 3 were waited for; matrix products, arithmetic and copies ran while one was open for 0% of the time, Pallas kernels for 5%

profile of v4, /device:TPU:1, one launch (start us, length us, event | category | flops | bytes accessed | tf_op | source)
XLA Modules:
  0.0 51.8 jit_solution(1230090939059583694)
XLA Ops:
  0.6 0.0 copy-start
  0.6 0.0 copy-start.2
  0.7 0.0 copy-start.3
  0.7 0.0 copy-start.1
  0.7 5.9 %run_sums.2 = bf16[128,4,128]{2,1,0:T(4,128)(2,1)} custom-call(s32[32,128]{1,0:T(8,128)} %bitcast.9, s32[1,128]{1,0:T(1,128)} %bitcast.11, s32[1,128]{1,0:T(1,128)} %bitcast.13, bf16[4096,1536]{1,0:T(8,128)(2,1)} %refs_3_.1), custom_call_target="tpu_custom_call" | custom-call | flops 3221225472 | bytes 12582912 | tf_op jit(solution)/shard_map/run_sums/pallas_call | solution.py:115
  6.5 0.0 copy-done.1
  6.5 3.8 %collective-permute-start = (bf16[16,1536]{1,0:T(8,128)(2,1)S(1)}, bf16[16,1536]{1,0:T(8,128)(2,1)S(1)}, u32[]{:S(2)}, u32[]{:S(2)}) collective-permute-start(bf16[16,1536]{1,0:T(8,128)(2,1)S(1)} %copy-done.1), channel_id=1, source_target_pairs={{0,2},{1,3},{2,0},{3,1},{4,6},{5,7},{6,4},{7,5},{8,10},{9,11},{10,... | collective-permute-start | bytes 147464 | tf_op jit(solution)/shard_map/ppermute | solution.py:290
  10.4 8.8 %all-to-all-start.1 = ((bf16[128,4,128]{2,1,0:T(4,128)(2,1)}), bf16[128,4,128]{2,1,0:T(4,128)(2,1)S(1)}, u32[]{:S(2)}, u32[]{:S(2)}) async-start(bf16[128,4,128]{2,1,0:T(4,128)(2,1)} %run_sums.2), calls=%async_computation.1 | async-start | bytes 262144 | tf_op jit(solution)/shard_map/all_to_all | solution.py:286
  19.2 0.0 collective-permute-done
  19.2 1.5 %collective-permute-start.1 = (bf16[32,1536]{1,0:T(8,128)(2,1)S(1)}, bf16[32,1536]{1,0:T(8,128)(2,1)S(1)}, u32[]{:S(2)}, u32[]{:S(2)}) collective-permute-start(bf16[32,1536]{1,0:T(8,128)(2,1)S(1)} %get-tuple-element.80), channel_id=1, source_target_pairs={{0,4},{1,5},{2,6},{3,7},{4,0},{5,1},{6,2},{7,3},{8,12},{9,13},{10,... | collective-permute-start | bytes 294920 | tf_op jit(solution)/shard_map/ppermute | solution.py:290
  20.7 2.4 %collective-permute-start.2 = (bf16[32,1536]{1,0:T(8,128)(2,1)S(1)}, bf16[32,1536]{1,0:T(8,128)(2,1)S(1)}, u32[]{:S(2)}, u32[]{:S(2)}) collective-permute-start(bf16[32,1536]{1,0:T(8,128)(2,1)S(1)} %get-tuple-element.80), channel_id=1, source_target_pairs={{0,8},{1,9},{2,10},{3,11},{4,12},{5,13},{6,14},{7,15},{8,0},{9,1},... | collective-permute-start | bytes 294920 | tf_op jit(solution)/shard_map/ppermute | solution.py:290
  23.1 0.1 collective-permute-start.3
  23.2 6.0 %all-to-all-done.1.refs_0_ = bf16[128,4,128]{2,1,0:T(4,128)(2,1)S(1)} async-done(((bf16[128,4,128]{2,1,0:T(4,128)(2,1)}), bf16[128,4,128]{2,1,0:T(4,128)(2,1)S(1)}, u32[]{:S(2)}, u32[]{:S(2)}) %all-to-all-start.1) | async-done | bytes 131104 | tf_op jit(solution)/shard_map/all_to_all | solution.py:286
  29.1 2.5 %means.2 = (bf16[128,16,128]{2,1,0:T(8,128)(2,1)}, f32[256,128]{1,0:T(8,128)S(1)}, s32[1]{0:T(128)}) custom-call(bf16[128,4,128]{2,1,0:T(4,128)(2,1)S(1)} %all-to-all-done.1.refs_0_), custom_call_target="tpu_custom_call" | custom-call | tf_op jit(solution)/shard_map/means/pallas_call | solution.py:216
  31.6 0.0 copy-done
  31.6 0.0 copy-done.2
  31.6 0.0 copy-done.3
  31.6 0.7 %while.12 = (s32[]{:T(128)}, bf16[128,16,128]{2,1,0:T(8,128)(2,1)}, f32[256,128]{1,0:T(8,128)S(1)}, s32[1]{0:T(128)}, s32[32,128]{1,0:T(8,128)S(1)}, /*index=5*/...) while((s32[]{:T(128)}, bf16[128,16,128]{2,1,0:T(8,128)(2,1)}, ...), condition=%wide.region_1.0_spmd, body=%wide.region_0.0_spmd.sunk | while | flops 3221225472 | bytes 13238417 | solution.py:314
  32.3 4.4 %all-to-all-start.2 = ((bf16[128,16,128]{2,1,0:T(8,128)(2,1)}), bf16[128,16,128]{2,1,0:T(8,128)(2,1)S(1)}, u32[]{:S(2)}, u32[]{:S(2)}) async-start(bf16[128,16,128]{2,1,0:T(8,128)(2,1)} %get-tuple-element.59), calls=%async_computation.2 | async-start | bytes 1048576 | tf_op jit(solution)/shard_map/all_to_all | solution.py:286
  36.7 0.0 collective-permute-done.1
  36.7 0.0 collective-permute-done.2
  36.7 0.0 collective-permute-done.3
  36.8 1.1 %collective-permute-start.4 = (bf16[128,1536]{1,0:T(8,128)(2,1)S(1)}, bf16[128,1536]{1,0:T(8,128)(2,1)S(1)}, u32[]{:S(2)}, u32[]{:S(2)}) collective-permute-start(bf16[128,1536]{1,0:T(8,128)(2,1)S(1)} %constant_dynamic-update-slice_fusion.2.refs_1_), channel_id=1, source_target_pairs={{0,1},{1,0},{2,3},{3,2},{4,5},{5,4},{6,7},{7,6},{8,9},{9,8},{10,11... | collective-permute-start | bytes 1179656 | tf_op jit(solution)/shard_map/ppermute | solution.py:290
  37.9 1.3 %collective-permute-done.4.refs_2_ = bf16[128,1536]{1,0:T(8,128)(2,1)S(1)} collective-permute-done((bf16[128,1536]{1,0:T(8,128)(2,1)S(1)}, bf16[128,1536]{1,0:T(8,128)(2,1)S(1)}, u32[]{:S(2)}, u32[]{:S(2)}) %collective-permute-start.4) | collective-permute-done | bytes 393248 | tf_op jit(solution)/shard_map/ppermute | solution.py:290
  39.3 11.0 %all-to-all-done.2.refs_0_ = bf16[128,16,128]{2,1,0:T(8,128)(2,1)S(1)} async-done(((bf16[128,16,128]{2,1,0:T(8,128)(2,1)}), bf16[128,16,128]{2,1,0:T(8,128)(2,1)S(1)}, u32[]{:S(2)}, u32[]{:S(2)}) %all-to-all-start.2) | async-done | bytes 524320 | tf_op jit(solution)/shard_map/all_to_all | solution.py:286
  50.3 1.5 %finish.1 = (bf16[128,1536]{1,0:T(8,128)(2,1)}, f32[1,128]{1,0:T(1,128)}, bf16[16,1536]{1,0:T(8,128)(2,1)}) custom-call(bf16[128,16,128]{2,1,0:T(8,128)(2,1)S(1)} %all-to-all-done.2.refs_0_, bf16[128,1536]{1,0:T(8,128)(2,1)S(1)} %constant_dynamic-update-slice_fusion.2.refs_1_, bf16[128,1536]{1,0:T(8,128)(2,1)S(1)} %collective-permute-done.4.refs_2_), custom_call_target="tpu_custom_call" | custom-call | tf_op jit(solution)/shard_map/finish/pallas_call | solution.py:270
  (5 shorter events, 0.0 us)
Async XLA Ops:
  0.6 31.0 %copy-start = (s32[4096]{0:T(1024)S(1)}, s32[4096]{0:T(1024)}, u32[]{:S(2)}) copy-start(s32[4096]{0:T(1024)} %param.8) | copy-start | bytes 49156
  0.6 31.0 %copy-start.2 = (s32[128]{0:T(128)S(1)}, s32[128]{0:T(128)}, u32[]{:S(2)}) copy-start(s32[128]{0:T(128)} %param.9) | copy-start | bytes 1540
  0.7 31.0 %copy-start.3 = (s32[128,1]{0,1:T(1,128)S(1)}, s32[128,1]{0,1:T(1,128)}, u32[]{:S(2)}) copy-start(s32[128,1]{0,1:T(1,128)} %param.11) | copy-start | bytes 1540
  0.7 5.9 %copy-start.1 = (bf16[16,1536]{1,0:T(8,128)(2,1)S(1)}, bf16[16,1536]{1,0:T(8,128)(2,1)}, u32[]{:S(2)}) copy-start(bf16[16,1536]{1,0:T(8,128)(2,1)} %param.10) | copy-start | bytes 147460
  6.5 12.7 %collective-permute-start = (bf16[16,1536]{1,0:T(8,128)(2,1)S(1)}, bf16[16,1536]{1,0:T(8,128)(2,1)S(1)}, u32[]{:S(2)}, u32[]{:S(2)}) collective-permute-start(bf16[16,1536]{1,0:T(8,128)(2,1)S(1)} %copy-done.1), channel_id=1, source_target_pairs={{0,2},{1,3},{2,0},{3,1},{4,6},{5,7},{6,4},{7,5},{8,10},{9,11},{10,... | collective-permute-start | bytes 147464 | tf_op jit(solution)/shard_map/ppermute | solution.py:290
  10.4 18.7 %all-to-all-start.1 = ((bf16[128,4,128]{2,1,0:T(4,128)(2,1)}), bf16[128,4,128]{2,1,0:T(4,128)(2,1)S(1)}, u32[]{:S(2)}, u32[]{:S(2)}) async-start(bf16[128,4,128]{2,1,0:T(4,128)(2,1)} %run_sums.2), calls=%async_computation.1 | async-start | bytes 262144 | tf_op jit(solution)/shard_map/all_to_all | solution.py:286
  19.2 17.5 %collective-permute-start.1 = (bf16[32,1536]{1,0:T(8,128)(2,1)S(1)}, bf16[32,1536]{1,0:T(8,128)(2,1)S(1)}, u32[]{:S(2)}, u32[]{:S(2)}) collective-permute-start(bf16[32,1536]{1,0:T(8,128)(2,1)S(1)} %get-tuple-element.80), channel_id=1, source_target_pairs={{0,4},{1,5},{2,6},{3,7},{4,0},{5,1},{6,2},{7,3},{8,12},{9,13},{10,... | collective-permute-start | bytes 294920 | tf_op jit(solution)/shard_map/ppermute | solution.py:290
  20.7 16.0 %collective-permute-start.2 = (bf16[32,1536]{1,0:T(8,128)(2,1)S(1)}, bf16[32,1536]{1,0:T(8,128)(2,1)S(1)}, u32[]{:S(2)}, u32[]{:S(2)}) collective-permute-start(bf16[32,1536]{1,0:T(8,128)(2,1)S(1)} %get-tuple-element.80), channel_id=1, source_target_pairs={{0,8},{1,9},{2,10},{3,11},{4,12},{5,13},{6,14},{7,15},{8,0},{9,1},... | collective-permute-start | bytes 294920 | tf_op jit(solution)/shard_map/ppermute | solution.py:290
  23.1 13.7 %collective-permute-start.3 = (bf16[32,1536]{1,0:T(8,128)(2,1)S(1)}, bf16[32,1536]{1,0:T(8,128)(2,1)S(1)}, u32[]{:S(2)}, u32[]{:S(2)}) collective-permute-start(bf16[32,1536]{1,0:T(8,128)(2,1)S(1)} %get-tuple-element.80), channel_id=1, source_target_pairs={{0,12},{1,13},{2,14},{3,15},{4,8},{5,9},{6,10},{7,11},{8,4},{9,5},... | collective-permute-start | bytes 294920 | tf_op jit(solution)/shard_map/ppermute | solution.py:290
  32.3 18.0 %all-to-all-start.2 = ((bf16[128,16,128]{2,1,0:T(8,128)(2,1)}), bf16[128,16,128]{2,1,0:T(8,128)(2,1)S(1)}, u32[]{:S(2)}, u32[]{:S(2)}) async-start(bf16[128,16,128]{2,1,0:T(8,128)(2,1)} %get-tuple-element.59), calls=%async_computation.2 | async-start | bytes 1048576 | tf_op jit(solution)/shard_map/all_to_all | solution.py:286
  36.8 2.5 %collective-permute-start.4 = (bf16[128,1536]{1,0:T(8,128)(2,1)S(1)}, bf16[128,1536]{1,0:T(8,128)(2,1)S(1)}, u32[]{:S(2)}, u32[]{:S(2)}) collective-permute-start(bf16[128,1536]{1,0:T(8,128)(2,1)S(1)} %constant_dynamic-update-slice_fusion.2.refs_1_), channel_id=1, source_target_pairs={{0,1},{1,0},{2,3},{3,2},{4,5},{5,4},{6,7},{7,6},{8,9},{9,8},{10,11... | collective-permute-start | bytes 1179656 | tf_op jit(solution)/shard_map/ppermute | solution.py:290

commit v5 on v4

--- a/solution.py
+++ b/solution.py
@@ -12,6 +12,7 @@
 LANES = 128
 FIELDS = 16
 COLS = 12
+HALF = 7
 BLOCK = 256
 
 
@@ -140,7 +141,7 @@
         runs_ref, before_ref, *refs = refs
     else:
         runs_ref, *refs = refs
-    out_ref, acc_ref, rounds_ref, wide_ref, field_ref, send_ref = refs
+    out_ref, acc_ref, rounds_ref, wide_ref, field_ref, send_ref, dense_ref = refs
     wide_ref[...] = runs_ref[...].reshape(4 * LANES, LANES).astype(F32)
     for q in range(4):
         field_ref[q * LANES : (q + 1) * LANES, :] = wide_ref[pl.ds(q, LANES, stride=4), :].T
@@ -201,7 +202,11 @@
     send_ref[pl.ds(13, 16, stride=16), :] = jnp.concatenate(
         [level2[:, LANES:], jnp.zeros((16, 2 * LANES - COLS * 16), F32)], axis=1
     )
-    block = send_ref[...].astype(BF16).reshape(16, 16, LANES)
+    for t in range(2 * HALF):
+        half, place = t // HALF, t % HALF
+        dense_ref[place, pl.ds(half, 16, stride=2), :] = send_ref[pl.ds(t, 16, stride=16), :]
+    dense = jnp.concatenate([dense_ref[place] for place in range(HALF)], axis=1)
+    block = dense.astype(BF16).reshape(16, 2, HALF * LANES)
     for i in range(8):
         out_ref[i * 16 : (i + 1) * 16] = block
 
@@ -218,7 +223,7 @@
         in_specs=[vmem] * len(args),
         out_specs=[vmem, vmem, pl.BlockSpec(memory_space=pltpu.SMEM)],
         out_shape=[
-            jax.ShapeDtypeStruct((LANES, 16, LANES), BF16),
+            jax.ShapeDtypeStruct((LANES, 2, HALF * LANES), BF16),
             jax.ShapeDtypeStruct((16 * FIELDS, LANES), F32),
             jax.ShapeDtypeStruct((1,), jnp.int32),
         ],
@@ -226,6 +231,7 @@
             pltpu.VMEM((4 * LANES, LANES), F32),
             pltpu.VMEM((4 * LANES, LANES), F32),
             pltpu.VMEM((16 * FIELDS, LANES), F32),
+            pltpu.VMEM((HALF, 32, LANES), F32),
         ],
         compiler_params=pltpu.CompilerParams(vmem_limit_bytes=8 << 20),
         name="means",
@@ -234,13 +240,19 @@
 
 def finish_kernel(parts, rows_ref, *refs):
     centre_refs, (level1_ref, nearest_ref, level2_ref, wide_ref) = refs[:parts], refs[parts:]
-    wide_ref[...] = rows_ref[...].reshape(LANES * 16, LANES).astype(F32)
+    rows = rows_ref[...].reshape(2 * LANES, HALF * LANES).astype(F32)
+    for place in range(HALF):
+        wide_ref[place] = rows[:, place * LANES : (place + 1) * LANES]
+
+    def taken(t):
+        return wide_ref[t % HALF, pl.ds(t // HALF, LANES, stride=2), :]
+
     width = COLS * LANES
     crosses = [None] * parts
     norm = jnp.zeros((1, LANES), F32)
     for f in range(COLS):
         columns = slice(f * LANES, (f + 1) * LANES)
-        block = wide_ref[pl.ds(f, LANES, stride=16), :]
+        block = taken(f)
         level1_ref[:, columns] = block.T.astype(BF16)
         norm = norm + jnp.sum(block * block, axis=0, keepdims=True)
         small = block.astype(BF16)
@@ -256,7 +268,7 @@
         best = least if best is None else jnp.minimum(best, least)
     nearest_ref[...] = best
     for half in range(2):
-        block = wide_ref[pl.ds(12 + half, LANES, stride=16), :].T
+        block = taken(12 + half).T
         for f in range(8 * half, min(COLS, 8 * half + 8)):
             level2_ref[:, f * LANES : (f + 1) * LANES] = block[(f % 8) * 16 : (f % 8 + 1) * 16, :].astype(BF16)
 
@@ -276,7 +288,7 @@
             jax.ShapeDtypeStruct((1, LANES), F32),
             jax.ShapeDtypeStruct((16, COLS * LANES), BF16),
         ],
-        scratch_shapes=[pltpu.VMEM((LANES * 16, LANES), F32)],
+        scratch_shapes=[pltpu.VMEM((HALF, 2 * LANES, LANES), F32)],
         compiler_params=pltpu.CompilerParams(vmem_limit_bytes=8 << 20),
         name="finish",
     )(rows, *centres)

time: 52 us -> 51.3 us (0.987)
  starting transfers between devices: 22.1 us -> 21.1 us
    all_to_all x2, starting transfers between devices: 13.2 us -> 12.6 us  [exchange(): return lax.all_to_all(value, BOTH, 0, 0, tiled=True)]
where the time goes in v5:
time: 51.3 us; the launch traced here: 51.1 us
  starting transfers between devices  21.1 us (41%)
  waiting for transfers between devices  18.5 us (36%)
  Pallas kernels  9.97 us (19%)
  between operations  0.8 us (2%)
  loops' own time  0.65 us (1%)
    all_to_all x2, waiting for transfers between devices, exchange(): return lax.all_to_all(value, BOTH, 0, 0, tiled=True)  17.1 us
    all_to_all x2, starting transfers between devices, exchange(): return lax.all_to_all(value, BOTH, 0, 0, tiled=True)  12.6 us
    ppermute x5, starting transfers between devices, swapped(): return lax.ppermute(value, 'cent', [(i, i ^ mask) for i in range(16)])  8.46 us
    pallas_call x1, Pallas kernels, run_sums(): pl.pallas_call(kernel, in_specs=specs, out_specs=vmem, out_shape=jax.Shap...  5.85 us
    pallas_call x1, Pallas kernels, means(): pl.pallas_call(kernel, in_specs=[vmem] * len(args), out_specs=[vmem, vmem...  2.49 us
    pallas_call x1, Pallas kernels, finish(): pl.pallas_call(kernel, in_specs=[vmem] * (1 + len(centres)), out_specs=[v...  1.62 us
    ppermute x5, waiting for transfers between devices, swapped(): return lax.ppermute(value, 'cent', [(i, i ^ mask) for i in range(16)])  1.36 us
  transfers between devices with their start and end apart: 7, of which 3 were waited for; matrix products, arithmetic and copies ran while one was open for 0% of the time, Pallas kernels for 5%

profile of v5, /device:TPU:1, one launch (start us, length us, event | category | flops | bytes accessed | tf_op | source)
XLA Modules:
  0.0 51.1 jit_solution(18216077759385848126)
XLA Ops:
  0.6 0.0 copy-start.3
  0.6 0.0 copy-start.2
  0.7 0.0 copy-start
  0.7 0.0 copy-start.1
  0.7 5.9 %run_sums.2 = bf16[128,4,128]{2,1,0:T(4,128)(2,1)} custom-call(s32[32,128]{1,0:T(8,128)} %bitcast.9, s32[1,128]{1,0:T(1,128)} %bitcast.11, s32[1,128]{1,0:T(1,128)} %bitcast.13, bf16[4096,1536]{1,0:T(8,128)(2,1)} %refs_3_.1), custom_call_target="tpu_custom_call" | custom-call | flops 3221225472 | bytes 12582912 | tf_op jit(solution)/shard_map/run_sums/pallas_call | solution.py:116
  6.5 0.0 copy-done.1
  6.5 3.8 %collective-permute-start = (bf16[16,1536]{1,0:T(8,128)(2,1)S(1)}, bf16[16,1536]{1,0:T(8,128)(2,1)S(1)}, u32[]{:S(2)}, u32[]{:S(2)}) collective-permute-start(bf16[16,1536]{1,0:T(8,128)(2,1)S(1)} %copy-done.1), channel_id=1, source_target_pairs={{0,2},{1,3},{2,0},{3,1},{4,6},{5,7},{6,4},{7,5},{8,10},{9,11},{10,... | collective-permute-start | bytes 147464 | tf_op jit(solution)/shard_map/ppermute | solution.py:302
  10.4 8.8 %all-to-all-start.1 = ((bf16[128,4,128]{2,1,0:T(4,128)(2,1)}), bf16[128,4,128]{2,1,0:T(4,128)(2,1)S(1)}, u32[]{:S(2)}, u32[]{:S(2)}) async-start(bf16[128,4,128]{2,1,0:T(4,128)(2,1)} %run_sums.2), calls=%async_computation.1 | async-start | bytes 262144 | tf_op jit(solution)/shard_map/all_to_all | solution.py:298
  19.2 0.0 collective-permute-done
  19.2 2.7 %collective-permute-start.3 = (bf16[32,1536]{1,0:T(8,128)(2,1)S(1)}, bf16[32,1536]{1,0:T(8,128)(2,1)S(1)}, u32[]{:S(2)}, u32[]{:S(2)}) collective-permute-start(bf16[32,1536]{1,0:T(8,128)(2,1)S(1)} %get-tuple-element.80), channel_id=1, source_target_pairs={{0,12},{1,13},{2,14},{3,15},{4,8},{5,9},{6,10},{7,11},{8,4},{9,5},... | collective-permute-start | bytes 294920 | tf_op jit(solution)/shard_map/ppermute | solution.py:302
  21.9 0.6 %collective-permute-start.2 = (bf16[32,1536]{1,0:T(8,128)(2,1)S(1)}, bf16[32,1536]{1,0:T(8,128)(2,1)S(1)}, u32[]{:S(2)}, u32[]{:S(2)}) collective-permute-start(bf16[32,1536]{1,0:T(8,128)(2,1)S(1)} %get-tuple-element.80), channel_id=1, source_target_pairs={{0,8},{1,9},{2,10},{3,11},{4,12},{5,13},{6,14},{7,15},{8,0},{9,1},... | collective-permute-start | bytes 294920 | tf_op jit(solution)/shard_map/ppermute | solution.py:302
  22.5 0.1 collective-permute-start.1
  22.6 6.8 %all-to-all-done.1.refs_0_ = bf16[128,4,128]{2,1,0:T(4,128)(2,1)S(1)} async-done(((bf16[128,4,128]{2,1,0:T(4,128)(2,1)}), bf16[128,4,128]{2,1,0:T(4,128)(2,1)S(1)}, u32[]{:S(2)}, u32[]{:S(2)}) %all-to-all-start.1) | async-done | bytes 131104 | tf_op jit(solution)/shard_map/all_to_all | solution.py:298
  29.4 2.5 %means.2 = (bf16[128,2,896]{2,1,0:T(2,128)(2,1)}, f32[256,128]{1,0:T(8,128)S(1)}, s32[1]{0:T(128)}) custom-call(bf16[128,4,128]{2,1,0:T(4,128)(2,1)S(1)} %all-to-all-done.1.refs_0_), custom_call_target="tpu_custom_call" | custom-call | tf_op jit(solution)/shard_map/means/pallas_call | solution.py:221
  31.9 0.0 copy-done.3
  31.9 0.0 copy-done.2
  31.9 0.0 copy-done
  31.9 0.7 %while.12 = (s32[]{:T(128)}, bf16[128,2,896]{2,1,0:T(2,128)(2,1)}, f32[256,128]{1,0:T(8,128)S(1)}, s32[1]{0:T(128)}, s32[32,128]{1,0:T(8,128)S(1)}, /*index=5*/s...) while((s32[]{:T(128)}, bf16[128,2,896]{2,1,0:T(2,128)(2,1)}, ...), condition=%wide.region_1.0_spmd, body=%wide.region_0.0_spmd.sunk | while | flops 3221225472 | bytes 13238417 | solution.py:326
  32.6 3.8 %all-to-all-start.2 = ((bf16[128,2,896]{2,1,0:T(2,128)(2,1)}), bf16[128,2,896]{2,1,0:T(2,128)(2,1)S(1)}, u32[]{:S(2)}, u32[]{:S(2)}) async-start(bf16[128,2,896]{2,1,0:T(2,128)(2,1)} %get-tuple-element.59), calls=%async_computation.2 | async-start | bytes 917504 | tf_op jit(solution)/shard_map/all_to_all | solution.py:298
  36.4 0.0 collective-permute-done.1
  36.4 0.0 collective-permute-done.2
  36.4 0.0 collective-permute-done.3
  36.5 1.3 %collective-permute-start.4 = (bf16[128,1536]{1,0:T(8,128)(2,1)S(1)}, bf16[128,1536]{1,0:T(8,128)(2,1)S(1)}, u32[]{:S(2)}, u32[]{:S(2)}) collective-permute-start(bf16[128,1536]{1,0:T(8,128)(2,1)S(1)} %constant_dynamic-update-slice_fusion.2.refs_1_), channel_id=1, source_target_pairs={{0,1},{1,0},{2,3},{3,2},{4,5},{5,4},{6,7},{7,6},{8,9},{9,8},{10,11... | collective-permute-start | bytes 1179656 | tf_op jit(solution)/shard_map/ppermute | solution.py:302
  37.7 1.3 %collective-permute-done.4.refs_2_ = bf16[128,1536]{1,0:T(8,128)(2,1)S(1)} collective-permute-done((bf16[128,1536]{1,0:T(8,128)(2,1)S(1)}, bf16[128,1536]{1,0:T(8,128)(2,1)S(1)}, u32[]{:S(2)}, u32[]{:S(2)}) %collective-permute-start.4) | collective-permute-done | bytes 393248 | tf_op jit(solution)/shard_map/ppermute | solution.py:302
  39.1 10.3 %all-to-all-done.2.refs_0_ = bf16[128,2,896]{2,1,0:T(2,128)(2,1)S(1)} async-done(((bf16[128,2,896]{2,1,0:T(2,128)(2,1)}), bf16[128,2,896]{2,1,0:T(2,128)(2,1)S(1)}, u32[]{:S(2)}, u32[]{:S(2)}) %all-to-all-start.2) | async-done | bytes 458784 | tf_op jit(solution)/shard_map/all_to_all | solution.py:298
  49.4 1.6 %finish.1 = (bf16[128,1536]{1,0:T(8,128)(2,1)}, f32[1,128]{1,0:T(1,128)}, bf16[16,1536]{1,0:T(8,128)(2,1)}) custom-call(bf16[128,2,896]{2,1,0:T(2,128)(2,1)S(1)} %all-to-all-done.2.refs_0_, bf16[128,1536]{1,0:T(8,128)(2,1)S(1)} %constant_dynamic-update-slice_fusion.2.refs_1_, bf16[128,1536]{1,0:T(8,128)(2,1)S(1)} %collective-permute-done.4.refs_2_), custom_call_target="tpu_custom_call" | custom-call | tf_op jit(solution)/shard_map/finish/pallas_call | solution.py:282
  (5 shorter events, 0.0 us)
Async XLA Ops:
  0.6 31.2 %copy-start.3 = (s32[128,1]{0,1:T(1,128)S(1)}, s32[128,1]{0,1:T(1,128)}, u32[]{:S(2)}) copy-start(s32[128,1]{0,1:T(1,128)} %param.11) | copy-start | bytes 1540
  0.6 31.2 %copy-start.2 = (s32[128]{0:T(128)S(1)}, s32[128]{0:T(128)}, u32[]{:S(2)}) copy-start(s32[128]{0:T(128)} %param.9) | copy-start | bytes 1540
  0.7 31.2 %copy-start = (s32[4096]{0:T(1024)S(1)}, s32[4096]{0:T(1024)}, u32[]{:S(2)}) copy-start(s32[4096]{0:T(1024)} %param.8) | copy-start | bytes 49156
  0.7 5.9 %copy-start.1 = (bf16[16,1536]{1,0:T(8,128)(2,1)S(1)}, bf16[16,1536]{1,0:T(8,128)(2,1)}, u32[]{:S(2)}) copy-start(bf16[16,1536]{1,0:T(8,128)(2,1)} %param.10) | copy-start | bytes 147460
  6.5 12.7 %collective-permute-start = (bf16[16,1536]{1,0:T(8,128)(2,1)S(1)}, bf16[16,1536]{1,0:T(8,128)(2,1)S(1)}, u32[]{:S(2)}, u32[]{:S(2)}) collective-permute-start(bf16[16,1536]{1,0:T(8,128)(2,1)S(1)} %copy-done.1), channel_id=1, source_target_pairs={{0,2},{1,3},{2,0},{3,1},{4,6},{5,7},{6,4},{7,5},{8,10},{9,11},{10,... | collective-permute-start | bytes 147464 | tf_op jit(solution)/shard_map/ppermute | solution.py:302
  10.4 19.0 %all-to-all-start.1 = ((bf16[128,4,128]{2,1,0:T(4,128)(2,1)}), bf16[128,4,128]{2,1,0:T(4,128)(2,1)S(1)}, u32[]{:S(2)}, u32[]{:S(2)}) async-start(bf16[128,4,128]{2,1,0:T(4,128)(2,1)} %run_sums.2), calls=%async_computation.1 | async-start | bytes 262144 | tf_op jit(solution)/shard_map/all_to_all | solution.py:298
  19.2 17.2 %collective-permute-start.3 = (bf16[32,1536]{1,0:T(8,128)(2,1)S(1)}, bf16[32,1536]{1,0:T(8,128)(2,1)S(1)}, u32[]{:S(2)}, u32[]{:S(2)}) collective-permute-start(bf16[32,1536]{1,0:T(8,128)(2,1)S(1)} %get-tuple-element.80), channel_id=1, source_target_pairs={{0,12},{1,13},{2,14},{3,15},{4,8},{5,9},{6,10},{7,11},{8,4},{9,5},... | collective-permute-start | bytes 294920 | tf_op jit(solution)/shard_map/ppermute | solution.py:302
  21.9 14.5 %collective-permute-start.2 = (bf16[32,1536]{1,0:T(8,128)(2,1)S(1)}, bf16[32,1536]{1,0:T(8,128)(2,1)S(1)}, u32[]{:S(2)}, u32[]{:S(2)}) collective-permute-start(bf16[32,1536]{1,0:T(8,128)(2,1)S(1)} %get-tuple-element.80), channel_id=1, source_target_pairs={{0,8},{1,9},{2,10},{3,11},{4,12},{5,13},{6,14},{7,15},{8,0},{9,1},... | collective-permute-start | bytes 294920 | tf_op jit(solution)/shard_map/ppermute | solution.py:302
  22.5 13.9 %collective-permute-start.1 = (bf16[32,1536]{1,0:T(8,128)(2,1)S(1)}, bf16[32,1536]{1,0:T(8,128)(2,1)S(1)}, u32[]{:S(2)}, u32[]{:S(2)}) collective-permute-start(bf16[32,1536]{1,0:T(8,128)(2,1)S(1)} %get-tuple-element.80), channel_id=1, source_target_pairs={{0,4},{1,5},{2,6},{3,7},{4,0},{5,1},{6,2},{7,3},{8,12},{9,13},{10,... | collective-permute-start | bytes 294920 | tf_op jit(solution)/shard_map/ppermute | solution.py:302
  32.6 16.9 %all-to-all-start.2 = ((bf16[128,2,896]{2,1,0:T(2,128)(2,1)}), bf16[128,2,896]{2,1,0:T(2,128)(2,1)S(1)}, u32[]{:S(2)}, u32[]{:S(2)}) async-start(bf16[128,2,896]{2,1,0:T(2,128)(2,1)} %get-tuple-element.59), calls=%async_computation.2 | async-start | bytes 917504 | tf_op jit(solution)/shard_map/all_to_all | solution.py:298
  36.5 2.6 %collective-permute-start.4 = (bf16[128,1536]{1,0:T(8,128)(2,1)S(1)}, bf16[128,1536]{1,0:T(8,128)(2,1)S(1)}, u32[]{:S(2)}, u32[]{:S(2)}) collective-permute-start(bf16[128,1536]{1,0:T(8,128)(2,1)S(1)} %constant_dynamic-update-slice_fusion.2.refs_1_), channel_id=1, source_target_pairs={{0,1},{1,0},{2,3},{3,2},{4,5},{5,4},{6,7},{7,6},{8,9},{9,8},{10,11... | collective-permute-start | bytes 1179656 | tf_op jit(solution)/shard_map/ppermute | solution.py:302

commit v6 on v5

--- a/solution.py
+++ b/solution.py
@@ -306,12 +306,16 @@
     return lax.ppermute(value, "cent", [(i, (i + step) % 16) for i in range(16)])
 
 
+def across(value):
+    return lax.ppermute(value, BOTH, [(i, i ^ (4 * 16 + 2)) for i in range(128)])
+
+
 def body(points, assign, counts, level2, l2_assign):
     assign = assign.reshape(-1, LANES)
     counts = counts.reshape(1, LANES)
     labels = l2_assign.reshape(1, LANES)
     sums, level2 = lax.optimization_barrier((run_sums(points, assign, counts, labels, 0), level2))
-    near = jnp.concatenate([level2, swapped(level2, 2)], axis=0)
+    near = jnp.concatenate([level2, across(level2)], axis=0)
     runs = exchange(sums)
     centres = jnp.concatenate([near] + [swapped(near, mask) for mask in (4, 8, 12)], axis=0)
     send, acc, rounds = means(runs)

time: 51.3 us -> 50.7 us (0.988)
  starting transfers between devices: 21.1 us -> 20.5 us
    ppermute x5 -> x4, starting transfers between devices: 8.46 us -> 4.63 us  [swapped(): return lax.ppermute(value, 'cent', [(i, i ^ mask) for i in range(16)])]
    ppermute x0 -> x1, starting transfers between devices: none -> 3.64 us  [across(): return lax.ppermute(value, BOTH, [(i, i ^ 4 * 16 + 2) for i in range(128)])]
    ppermute x5 -> x4, waiting for transfers between devices: 1.36 us -> 1.36 us  [swapped(): return lax.ppermute(value, 'cent', [(i, i ^ mask) for i in range(16)])]
where the time goes in v6:
time: 50.7 us; the launch traced here: 50.5 us
  starting transfers between devices  20.5 us (40%)
  waiting for transfers between devices  18.5 us (36%)
  Pallas kernels  9.97 us (20%)
  between operations  0.8 us (2%)
  loops' own time  0.65 us (1%)
    all_to_all x2, waiting for transfers between devices, exchange(): return lax.all_to_all(value, BOTH, 0, 0, tiled=True)  17.1 us
    all_to_all x2, starting transfers between devices, exchange(): return lax.all_to_all(value, BOTH, 0, 0, tiled=True)  12.2 us
    pallas_call x1, Pallas kernels, run_sums(): pl.pallas_call(kernel, in_specs=specs, out_specs=vmem, out_shape=jax.Shap...  5.85 us
    ppermute x4, starting transfers between devices, swapped(): return lax.ppermute(value, 'cent', [(i, i ^ mask) for i in range(16)])  4.63 us
    ppermute x1, starting transfers between devices, across(): return lax.ppermute(value, BOTH, [(i, i ^ 4 * 16 + 2) for i in range(128)])  3.64 us
    pallas_call x1, Pallas kernels, means(): pl.pallas_call(kernel, in_specs=[vmem] * len(args), out_specs=[vmem, vmem...  2.49 us
    pallas_call x1, Pallas kernels, finish(): pl.pallas_call(kernel, in_specs=[vmem] * (1 + len(centres)), out_specs=[v...  1.63 us
    ppermute x4, waiting for transfers between devices, swapped(): return lax.ppermute(value, 'cent', [(i, i ^ mask) for i in range(16)])  1.36 us
  transfers between devices with their start and end apart: 7, of which 3 were waited for; matrix products, arithmetic and copies ran while one was open for 0% of the time, Pallas kernels for 5%

profile of v6, /device:TPU:1, one launch (start us, length us, event | category | flops | bytes accessed | tf_op | source)
XLA Modules:
  0.0 50.5 jit_solution(522507270411432452)
XLA Ops:
  0.6 0.0 copy-start.3
  0.6 0.0 copy-start.2
  0.7 0.0 copy-start
  0.7 0.0 copy-start.1
  0.7 5.9 %run_sums.2 = bf16[128,4,128]{2,1,0:T(4,128)(2,1)} custom-call(s32[32,128]{1,0:T(8,128)} %bitcast.9, s32[1,128]{1,0:T(1,128)} %bitcast.11, s32[1,128]{1,0:T(1,128)} %bitcast.13, bf16[4096,1536]{1,0:T(8,128)(2,1)} %refs_3_.1), custom_call_target="tpu_custom_call" | custom-call | flops 3221225472 | bytes 12582912 | tf_op jit(solution)/shard_map/run_sums/pallas_call | solution.py:116
  6.5 0.0 copy-done.1
  6.5 3.6 %collective-permute-start = (bf16[16,1536]{1,0:T(8,128)(2,1)S(1)}, bf16[16,1536]{1,0:T(8,128)(2,1)S(1)}, u32[]{:S(2)}, u32[]{:S(2)}) collective-permute-start(bf16[16,1536]{1,0:T(8,128)(2,1)S(1)} %copy-done.1), channel_id=1, source_target_pairs={{0,66},{1,67},{2,64},{3,65},{4,70},{5,71},{6,68},{7,69},{8,74},{9,... | collective-permute-start | bytes 147464 | tf_op jit(solution)/shard_map/ppermute | solution.py:310
  10.2 8.4 %all-to-all-start.1 = ((bf16[128,4,128]{2,1,0:T(4,128)(2,1)}), bf16[128,4,128]{2,1,0:T(4,128)(2,1)S(1)}, u32[]{:S(2)}, u32[]{:S(2)}) async-start(bf16[128,4,128]{2,1,0:T(4,128)(2,1)} %run_sums.2), calls=%async_computation.1 | async-start | bytes 262144 | tf_op jit(solution)/shard_map/all_to_all | solution.py:298
  18.6 0.0 collective-permute-done
  18.6 2.7 %collective-permute-start.3 = (bf16[32,1536]{1,0:T(8,128)(2,1)S(1)}, bf16[32,1536]{1,0:T(8,128)(2,1)S(1)}, u32[]{:S(2)}, u32[]{:S(2)}) collective-permute-start(bf16[32,1536]{1,0:T(8,128)(2,1)S(1)} %get-tuple-element.80), channel_id=1, source_target_pairs={{0,12},{1,13},{2,14},{3,15},{4,8},{5,9},{6,10},{7,11},{8,4},{9,5},... | collective-permute-start | bytes 294920 | tf_op jit(solution)/shard_map/ppermute | solution.py:302
  21.3 0.6 %collective-permute-start.2 = (bf16[32,1536]{1,0:T(8,128)(2,1)S(1)}, bf16[32,1536]{1,0:T(8,128)(2,1)S(1)}, u32[]{:S(2)}, u32[]{:S(2)}) collective-permute-start(bf16[32,1536]{1,0:T(8,128)(2,1)S(1)} %get-tuple-element.80), channel_id=1, source_target_pairs={{0,8},{1,9},{2,10},{3,11},{4,12},{5,13},{6,14},{7,15},{8,0},{9,1},... | collective-permute-start | bytes 294920 | tf_op jit(solution)/shard_map/ppermute | solution.py:302
  21.9 0.1 collective-permute-start.1
  22.0 6.8 %all-to-all-done.1.refs_0_ = bf16[128,4,128]{2,1,0:T(4,128)(2,1)S(1)} async-done(((bf16[128,4,128]{2,1,0:T(4,128)(2,1)}), bf16[128,4,128]{2,1,0:T(4,128)(2,1)S(1)}, u32[]{:S(2)}, u32[]{:S(2)}) %all-to-all-start.1) | async-done | bytes 131104 | tf_op jit(solution)/shard_map/all_to_all | solution.py:298
  28.8 2.5 %means.2 = (bf16[128,2,896]{2,1,0:T(2,128)(2,1)}, f32[256,128]{1,0:T(8,128)S(1)}, s32[1]{0:T(128)}) custom-call(bf16[128,4,128]{2,1,0:T(4,128)(2,1)S(1)} %all-to-all-done.1.refs_0_), custom_call_target="tpu_custom_call" | custom-call | tf_op jit(solution)/shard_map/means/pallas_call | solution.py:221
  31.3 0.0 copy-done.3
  31.3 0.0 copy-done.2
  31.3 0.0 copy-done
  31.3 0.7 %while.12 = (s32[]{:T(128)}, bf16[128,2,896]{2,1,0:T(2,128)(2,1)}, f32[256,128]{1,0:T(8,128)S(1)}, s32[1]{0:T(128)}, s32[32,128]{1,0:T(8,128)S(1)}, /*index=5*/s...) while((s32[]{:T(128)}, bf16[128,2,896]{2,1,0:T(2,128)(2,1)}, ...), condition=%wide.region_1.0_spmd, body=%wide.region_0.0_spmd.sunk | while | flops 3221225472 | bytes 13238417 | solution.py:330
  31.9 3.8 %all-to-all-start.2 = ((bf16[128,2,896]{2,1,0:T(2,128)(2,1)}), bf16[128,2,896]{2,1,0:T(2,128)(2,1)S(1)}, u32[]{:S(2)}, u32[]{:S(2)}) async-start(bf16[128,2,896]{2,1,0:T(2,128)(2,1)} %get-tuple-element.59), calls=%async_computation.2 | async-start | bytes 917504 | tf_op jit(solution)/shard_map/all_to_all | solution.py:298
  35.8 0.0 collective-permute-done.1
  35.8 0.0 collective-permute-done.2
  35.8 0.0 collective-permute-done.3
  35.9 1.3 %collective-permute-start.4 = (bf16[128,1536]{1,0:T(8,128)(2,1)S(1)}, bf16[128,1536]{1,0:T(8,128)(2,1)S(1)}, u32[]{:S(2)}, u32[]{:S(2)}) collective-permute-start(bf16[128,1536]{1,0:T(8,128)(2,1)S(1)} %constant_dynamic-update-slice_fusion.2.refs_1_), channel_id=1, source_target_pairs={{0,1},{1,0},{2,3},{3,2},{4,5},{5,4},{6,7},{7,6},{8,9},{9,8},{10,11... | collective-permute-start | bytes 1179656 | tf_op jit(solution)/shard_map/ppermute | solution.py:302
  37.1 1.3 %collective-permute-done.4.refs_2_ = bf16[128,1536]{1,0:T(8,128)(2,1)S(1)} collective-permute-done((bf16[128,1536]{1,0:T(8,128)(2,1)S(1)}, bf16[128,1536]{1,0:T(8,128)(2,1)S(1)}, u32[]{:S(2)}, u32[]{:S(2)}) %collective-permute-start.4) | collective-permute-done | bytes 393248 | tf_op jit(solution)/shard_map/ppermute | solution.py:302
  38.5 10.3 %all-to-all-done.2.refs_0_ = bf16[128,2,896]{2,1,0:T(2,128)(2,1)S(1)} async-done(((bf16[128,2,896]{2,1,0:T(2,128)(2,1)}), bf16[128,2,896]{2,1,0:T(2,128)(2,1)S(1)}, u32[]{:S(2)}, u32[]{:S(2)}) %all-to-all-start.2) | async-done | bytes 458784 | tf_op jit(solution)/shard_map/all_to_all | solution.py:298
  48.8 1.6 %finish.1 = (bf16[128,1536]{1,0:T(8,128)(2,1)}, f32[1,128]{1,0:T(1,128)}, bf16[16,1536]{1,0:T(8,128)(2,1)}) custom-call(bf16[128,2,896]{2,1,0:T(2,128)(2,1)S(1)} %all-to-all-done.2.refs_0_, bf16[128,1536]{1,0:T(8,128)(2,1)S(1)} %constant_dynamic-update-slice_fusion.2.refs_1_, bf16[128,1536]{1,0:T(8,128)(2,1)S(1)} %collective-permute-done.4.refs_2_), custom_call_target="tpu_custom_call" | custom-call | tf_op jit(solution)/shard_map/finish/pallas_call | solution.py:282
  (5 shorter events, 0.0 us)
Async XLA Ops:
  0.6 30.6 %copy-start.3 = (s32[128,1]{0,1:T(1,128)S(1)}, s32[128,1]{0,1:T(1,128)}, u32[]{:S(2)}) copy-start(s32[128,1]{0,1:T(1,128)} %param.11) | copy-start | bytes 1540
  0.6 30.6 %copy-start.2 = (s32[128]{0:T(128)S(1)}, s32[128]{0:T(128)}, u32[]{:S(2)}) copy-start(s32[128]{0:T(128)} %param.9) | copy-start | bytes 1540
  0.7 30.6 %copy-start = (s32[4096]{0:T(1024)S(1)}, s32[4096]{0:T(1024)}, u32[]{:S(2)}) copy-start(s32[4096]{0:T(1024)} %param.8) | copy-start | bytes 49156
  0.7 5.9 %copy-start.1 = (bf16[16,1536]{1,0:T(8,128)(2,1)S(1)}, bf16[16,1536]{1,0:T(8,128)(2,1)}, u32[]{:S(2)}) copy-start(bf16[16,1536]{1,0:T(8,128)(2,1)} %param.10) | copy-start | bytes 147460
  6.5 12.0 %collective-permute-start = (bf16[16,1536]{1,0:T(8,128)(2,1)S(1)}, bf16[16,1536]{1,0:T(8,128)(2,1)S(1)}, u32[]{:S(2)}, u32[]{:S(2)}) collective-permute-start(bf16[16,1536]{1,0:T(8,128)(2,1)S(1)} %copy-done.1), channel_id=1, source_target_pairs={{0,66},{1,67},{2,64},{3,65},{4,70},{5,71},{6,68},{7,69},{8,74},{9,... | collective-permute-start | bytes 147464 | tf_op jit(solution)/shard_map/ppermute | solution.py:310
  10.2 18.6 %all-to-all-start.1 = ((bf16[128,4,128]{2,1,0:T(4,128)(2,1)}), bf16[128,4,128]{2,1,0:T(4,128)(2,1)S(1)}, u32[]{:S(2)}, u32[]{:S(2)}) async-start(bf16[128,4,128]{2,1,0:T(4,128)(2,1)} %run_sums.2), calls=%async_computation.1 | async-start | bytes 262144 | tf_op jit(solution)/shard_map/all_to_all | solution.py:298
  18.6 17.2 %collective-permute-start.3 = (bf16[32,1536]{1,0:T(8,128)(2,1)S(1)}, bf16[32,1536]{1,0:T(8,128)(2,1)S(1)}, u32[]{:S(2)}, u32[]{:S(2)}) collective-permute-start(bf16[32,1536]{1,0:T(8,128)(2,1)S(1)} %get-tuple-element.80), channel_id=1, source_target_pairs={{0,12},{1,13},{2,14},{3,15},{4,8},{5,9},{6,10},{7,11},{8,4},{9,5},... | collective-permute-start | bytes 294920 | tf_op jit(solution)/shard_map/ppermute | solution.py:302
  21.3 14.5 %collective-permute-start.2 = (bf16[32,1536]{1,0:T(8,128)(2,1)S(1)}, bf16[32,1536]{1,0:T(8,128)(2,1)S(1)}, u32[]{:S(2)}, u32[]{:S(2)}) collective-permute-start(bf16[32,1536]{1,0:T(8,128)(2,1)S(1)} %get-tuple-element.80), channel_id=1, source_target_pairs={{0,8},{1,9},{2,10},{3,11},{4,12},{5,13},{6,14},{7,15},{8,0},{9,1},... | collective-permute-start | bytes 294920 | tf_op jit(solution)/shard_map/ppermute | solution.py:302
  21.9 13.9 %collective-permute-start.1 = (bf16[32,1536]{1,0:T(8,128)(2,1)S(1)}, bf16[32,1536]{1,0:T(8,128)(2,1)S(1)}, u32[]{:S(2)}, u32[]{:S(2)}) collective-permute-start(bf16[32,1536]{1,0:T(8,128)(2,1)S(1)} %get-tuple-element.80), channel_id=1, source_target_pairs={{0,4},{1,5},{2,6},{3,7},{4,0},{5,1},{6,2},{7,3},{8,12},{9,13},{10,... | collective-permute-start | bytes 294920 | tf_op jit(solution)/shard_map/ppermute | solution.py:302
  31.9 16.9 %all-to-all-start.2 = ((bf16[128,2,896]{2,1,0:T(2,128)(2,1)}), bf16[128,2,896]{2,1,0:T(2,128)(2,1)S(1)}, u32[]{:S(2)}, u32[]{:S(2)}) async-start(bf16[128,2,896]{2,1,0:T(2,128)(2,1)} %get-tuple-element.59), calls=%async_computation.2 | async-start | bytes 917504 | tf_op jit(solution)/shard_map/all_to_all | solution.py:298
  35.9 2.6 %collective-permute-start.4 = (bf16[128,1536]{1,0:T(8,128)(2,1)S(1)}, bf16[128,1536]{1,0:T(8,128)(2,1)S(1)}, u32[]{:S(2)}, u32[]{:S(2)}) collective-permute-start(bf16[128,1536]{1,0:T(8,128)(2,1)S(1)} %constant_dynamic-update-slice_fusion.2.refs_1_), channel_id=1, source_target_pairs={{0,1},{1,0},{2,3},{3,2},{4,5},{5,4},{6,7},{7,6},{8,9},{9,8},{10,11... | collective-permute-start | bytes 1179656 | tf_op jit(solution)/shard_map/ppermute | solution.py:302

commit v7 on v6

--- a/solution.py
+++ b/solution.py
@@ -314,7 +314,7 @@
     assign = assign.reshape(-1, LANES)
     counts = counts.reshape(1, LANES)
     labels = l2_assign.reshape(1, LANES)
-    sums, level2 = lax.optimization_barrier((run_sums(points, assign, counts, labels, 0), level2))
+    sums = run_sums(points, assign, counts, labels, 0)
     near = jnp.concatenate([level2, across(level2)], axis=0)
     runs = exchange(sums)
     centres = jnp.concatenate([near] + [swapped(near, mask) for mask in (4, 8, 12)], axis=0)

time: 50.7 us -> 50.6 us (level)
  transfers between devices with their start and end apart: 7 -> 7, of which waited for: 3 -> 3; matrix products, arithmetic and copies ran while one was open for 0% -> 0% of each run, Pallas kernels for 5% -> 16%
where the time goes in v7:
time: 50.6 us; the launch traced here: 50.4 us
  starting transfers between devices  20.5 us (41%)
  waiting for transfers between devices  18.5 us (37%)
  Pallas kernels  9.94 us (20%)
  between operations  0.81 us (2%)
  loops' own time  0.65 us (1%)
    all_to_all x2, waiting for transfers between devices, exchange(): return lax.all_to_all(value, BOTH, 0, 0, tiled=True)  17.1 us
    all_to_all x2, starting transfers between devices, exchange(): return lax.all_to_all(value, BOTH, 0, 0, tiled=True)  12.2 us
    pallas_call x1, Pallas kernels, run_sums(): pl.pallas_call(kernel, in_specs=specs, out_specs=vmem, out_shape=jax.Shap...  5.82 us
    ppermute x4, starting transfers between devices, swapped(): return lax.ppermute(value, 'cent', [(i, i ^ mask) for i in range(16)])  4.63 us
    ppermute x1, starting transfers between devices, across(): return lax.ppermute(value, BOTH, [(i, i ^ 4 * 16 + 2) for i in range(128)])  3.64 us
    pallas_call x1, Pallas kernels, means(): pl.pallas_call(kernel, in_specs=[vmem] * len(args), out_specs=[vmem, vmem...  2.49 us
    pallas_call x1, Pallas kernels, finish(): pl.pallas_call(kernel, in_specs=[vmem] * (1 + len(centres)), out_specs=[v...  1.62 us
    ppermute x4, waiting for transfers between devices, swapped(): return lax.ppermute(value, 'cent', [(i, i ^ mask) for i in range(16)])  1.36 us
  transfers between devices with their start and end apart: 7, of which 3 were waited for; matrix products, arithmetic and copies ran while one was open for 0% of the time, Pallas kernels for 16%

profile of v7, /device:TPU:1, one launch (start us, length us, event | category | flops | bytes accessed | tf_op | source)
XLA Modules:
  0.0 50.4 jit_solution(1816080439810184805)
XLA Ops:
  0.6 0.0 copy-start.1
  0.6 0.0 copy-start.3
  0.7 0.0 copy-start.2
  0.7 0.0 copy-start
  0.7 3.6 %collective-permute-start = (bf16[16,1536]{1,0:T(8,128)(2,1)}, bf16[16,1536]{1,0:T(8,128)(2,1)S(1)}, u32[]{:S(2)}, u32[]{:S(2)}) collective-permute-start(bf16[16,1536]{1,0:T(8,128)(2,1)} %param.10), channel_id=1, source_target_pairs={{0,66},{1,67},{2,64},{3,65},{4,70},{5,71},{6,68},{7,69},{8,74},{9,... | collective-permute-start | bytes 147464 | tf_op jit(solution)/shard_map/ppermute | solution.py:310
  4.3 5.8 %run_sums.2 = bf16[128,4,128]{2,1,0:T(4,128)(2,1)} custom-call(s32[32,128]{1,0:T(8,128)} %bitcast.9, s32[1,128]{1,0:T(1,128)} %bitcast.11, s32[1,128]{1,0:T(1,128)} %bitcast.13, bf16[4096,1536]{1,0:T(8,128)(2,1)} %refs_3_.1), custom_call_target="tpu_custom_call" | custom-call | flops 3221225472 | bytes 12582912 | tf_op jit(solution)/shard_map/run_sums/pallas_call | solution.py:116
  10.1 0.0 copy-done.1
  10.2 8.4 %all-to-all-start.1 = ((bf16[128,4,128]{2,1,0:T(4,128)(2,1)}), bf16[128,4,128]{2,1,0:T(4,128)(2,1)S(1)}, u32[]{:S(2)}, u32[]{:S(2)}) async-start(bf16[128,4,128]{2,1,0:T(4,128)(2,1)} %run_sums.2), calls=%async_computation.1 | async-start | bytes 262144 | tf_op jit(solution)/shard_map/all_to_all | solution.py:298
  18.6 0.0 collective-permute-done
  18.6 2.7 %collective-permute-start.3 = (bf16[32,1536]{1,0:T(8,128)(2,1)S(1)}, bf16[32,1536]{1,0:T(8,128)(2,1)S(1)}, u32[]{:S(2)}, u32[]{:S(2)}) collective-permute-start(bf16[32,1536]{1,0:T(8,128)(2,1)S(1)} %get-tuple-element.76), channel_id=1, source_target_pairs={{0,12},{1,13},{2,14},{3,15},{4,8},{5,9},{6,10},{7,11},{8,4},{9,5},... | collective-permute-start | bytes 294920 | tf_op jit(solution)/shard_map/ppermute | solution.py:302
  21.3 0.6 %collective-permute-start.2 = (bf16[32,1536]{1,0:T(8,128)(2,1)S(1)}, bf16[32,1536]{1,0:T(8,128)(2,1)S(1)}, u32[]{:S(2)}, u32[]{:S(2)}) collective-permute-start(bf16[32,1536]{1,0:T(8,128)(2,1)S(1)} %get-tuple-element.76), channel_id=1, source_target_pairs={{0,8},{1,9},{2,10},{3,11},{4,12},{5,13},{6,14},{7,15},{8,0},{9,1},... | collective-permute-start | bytes 294920 | tf_op jit(solution)/shard_map/ppermute | solution.py:302
  21.8 0.1 collective-permute-start.1
  21.9 6.8 %all-to-all-done.1.refs_0_ = bf16[128,4,128]{2,1,0:T(4,128)(2,1)S(1)} async-done(((bf16[128,4,128]{2,1,0:T(4,128)(2,1)}), bf16[128,4,128]{2,1,0:T(4,128)(2,1)S(1)}, u32[]{:S(2)}, u32[]{:S(2)}) %all-to-all-start.1) | async-done | bytes 131104 | tf_op jit(solution)/shard_map/all_to_all | solution.py:298
  28.7 2.5 %means.2 = (bf16[128,2,896]{2,1,0:T(2,128)(2,1)}, f32[256,128]{1,0:T(8,128)S(1)}, s32[1]{0:T(128)}) custom-call(bf16[128,4,128]{2,1,0:T(4,128)(2,1)S(1)} %all-to-all-done.1.refs_0_), custom_call_target="tpu_custom_call" | custom-call | tf_op jit(solution)/shard_map/means/pallas_call | solution.py:221
  31.2 0.0 copy-done.3
  31.2 0.0 copy-done.2
  31.3 0.0 copy-done
  31.3 0.7 %while.12 = (s32[]{:T(128)}, bf16[128,2,896]{2,1,0:T(2,128)(2,1)}, f32[256,128]{1,0:T(8,128)S(1)}, s32[1]{0:T(128)}, s32[32,128]{1,0:T(8,128)S(1)}, /*index=5*/s...) while((s32[]{:T(128)}, bf16[128,2,896]{2,1,0:T(2,128)(2,1)}, ...), condition=%wide.region_1.0_spmd, body=%wide.region_0.0_spmd.sunk | while | flops 3221225472 | bytes 13238417 | solution.py:330
  31.9 3.8 %all-to-all-start.2 = ((bf16[128,2,896]{2,1,0:T(2,128)(2,1)}), bf16[128,2,896]{2,1,0:T(2,128)(2,1)S(1)}, u32[]{:S(2)}, u32[]{:S(2)}) async-start(bf16[128,2,896]{2,1,0:T(2,128)(2,1)} %get-tuple-element.56), calls=%async_computation.2 | async-start | bytes 917504 | tf_op jit(solution)/shard_map/all_to_all | solution.py:298
  35.8 0.0 collective-permute-done.1
  35.8 0.0 collective-permute-done.2
  35.8 0.0 collective-permute-done.3
  35.8 1.3 %collective-permute-start.4 = (bf16[128,1536]{1,0:T(8,128)(2,1)S(1)}, bf16[128,1536]{1,0:T(8,128)(2,1)S(1)}, u32[]{:S(2)}, u32[]{:S(2)}) collective-permute-start(bf16[128,1536]{1,0:T(8,128)(2,1)S(1)} %constant_dynamic-update-slice_fusion.2.refs_1_), channel_id=1, source_target_pairs={{0,1},{1,0},{2,3},{3,2},{4,5},{5,4},{6,7},{7,6},{8,9},{9,8},{10,11... | collective-permute-start | bytes 1179656 | tf_op jit(solution)/shard_map/ppermute | solution.py:302
  37.1 1.3 %collective-permute-done.4.refs_2_ = bf16[128,1536]{1,0:T(8,128)(2,1)S(1)} collective-permute-done((bf16[128,1536]{1,0:T(8,128)(2,1)S(1)}, bf16[128,1536]{1,0:T(8,128)(2,1)S(1)}, u32[]{:S(2)}, u32[]{:S(2)}) %collective-permute-start.4) | collective-permute-done | bytes 393248 | tf_op jit(solution)/shard_map/ppermute | solution.py:302
  38.5 10.3 %all-to-all-done.2.refs_0_ = bf16[128,2,896]{2,1,0:T(2,128)(2,1)S(1)} async-done(((bf16[128,2,896]{2,1,0:T(2,128)(2,1)}), bf16[128,2,896]{2,1,0:T(2,128)(2,1)S(1)}, u32[]{:S(2)}, u32[]{:S(2)}) %all-to-all-start.2) | async-done | bytes 458784 | tf_op jit(solution)/shard_map/all_to_all | solution.py:298
  48.8 1.6 %finish.1 = (bf16[128,1536]{1,0:T(8,128)(2,1)}, f32[1,128]{1,0:T(1,128)}, bf16[16,1536]{1,0:T(8,128)(2,1)}) custom-call(bf16[128,2,896]{2,1,0:T(2,128)(2,1)S(1)} %all-to-all-done.2.refs_0_, bf16[128,1536]{1,0:T(8,128)(2,1)S(1)} %constant_dynamic-update-slice_fusion.2.refs_1_, bf16[128,1536]{1,0:T(8,128)(2,1)S(1)} %collective-permute-done.4.refs_2_), custom_call_target="tpu_custom_call" | custom-call | tf_op jit(solution)/shard_map/finish/pallas_call | solution.py:282
  (5 shorter events, 0.0 us)
Async XLA Ops:
  0.6 9.5 %copy-start.1 = (bf16[16,1536]{1,0:T(8,128)(2,1)S(1)}, bf16[16,1536]{1,0:T(8,128)(2,1)}, u32[]{:S(2)}) copy-start(bf16[16,1536]{1,0:T(8,128)(2,1)} %param.10) | copy-start | bytes 147460
  0.6 30.6 %copy-start.3 = (s32[128,1]{0,1:T(1,128)S(1)}, s32[128,1]{0,1:T(1,128)}, u32[]{:S(2)}) copy-start(s32[128,1]{0,1:T(1,128)} %param.11) | copy-start | bytes 1540
  0.7 30.6 %copy-start.2 = (s32[128]{0:T(128)S(1)}, s32[128]{0:T(128)}, u32[]{:S(2)}) copy-start(s32[128]{0:T(128)} %param.9) | copy-start | bytes 1540
  0.7 30.6 %copy-start = (s32[4096]{0:T(1024)S(1)}, s32[4096]{0:T(1024)}, u32[]{:S(2)}) copy-start(s32[4096]{0:T(1024)} %param.8) | copy-start | bytes 49156
  0.7 17.9 %collective-permute-start = (bf16[16,1536]{1,0:T(8,128)(2,1)}, bf16[16,1536]{1,0:T(8,128)(2,1)S(1)}, u32[]{:S(2)}, u32[]{:S(2)}) collective-permute-start(bf16[16,1536]{1,0:T(8,128)(2,1)} %param.10), channel_id=1, source_target_pairs={{0,66},{1,67},{2,64},{3,65},{4,70},{5,71},{6,68},{7,69},{8,74},{9,... | collective-permute-start | bytes 147464 | tf_op jit(solution)/shard_map/ppermute | solution.py:310
  10.2 18.6 %all-to-all-start.1 = ((bf16[128,4,128]{2,1,0:T(4,128)(2,1)}), bf16[128,4,128]{2,1,0:T(4,128)(2,1)S(1)}, u32[]{:S(2)}, u32[]{:S(2)}) async-start(bf16[128,4,128]{2,1,0:T(4,128)(2,1)} %run_sums.2), calls=%async_computation.1 | async-start | bytes 262144 | tf_op jit(solution)/shard_map/all_to_all | solution.py:298
  18.6 17.2 %collective-permute-start.3 = (bf16[32,1536]{1,0:T(8,128)(2,1)S(1)}, bf16[32,1536]{1,0:T(8,128)(2,1)S(1)}, u32[]{:S(2)}, u32[]{:S(2)}) collective-permute-start(bf16[32,1536]{1,0:T(8,128)(2,1)S(1)} %get-tuple-element.76), channel_id=1, source_target_pairs={{0,12},{1,13},{2,14},{3,15},{4,8},{5,9},{6,10},{7,11},{8,4},{9,5},... | collective-permute-start | bytes 294920 | tf_op jit(solution)/shard_map/ppermute | solution.py:302
  21.3 14.5 %collective-permute-start.2 = (bf16[32,1536]{1,0:T(8,128)(2,1)S(1)}, bf16[32,1536]{1,0:T(8,128)(2,1)S(1)}, u32[]{:S(2)}, u32[]{:S(2)}) collective-permute-start(bf16[32,1536]{1,0:T(8,128)(2,1)S(1)} %get-tuple-element.76), channel_id=1, source_target_pairs={{0,8},{1,9},{2,10},{3,11},{4,12},{5,13},{6,14},{7,15},{8,0},{9,1},... | collective-permute-start | bytes 294920 | tf_op jit(solution)/shard_map/ppermute | solution.py:302
  21.8 13.9 %collective-permute-start.1 = (bf16[32,1536]{1,0:T(8,128)(2,1)S(1)}, bf16[32,1536]{1,0:T(8,128)(2,1)S(1)}, u32[]{:S(2)}, u32[]{:S(2)}) collective-permute-start(bf16[32,1536]{1,0:T(8,128)(2,1)S(1)} %get-tuple-element.76), channel_id=1, source_target_pairs={{0,4},{1,5},{2,6},{3,7},{4,0},{5,1},{6,2},{7,3},{8,12},{9,13},{10,... | collective-permute-start | bytes 294920 | tf_op jit(solution)/shard_map/ppermute | solution.py:302
  31.9 16.9 %all-to-all-start.2 = ((bf16[128,2,896]{2,1,0:T(2,128)(2,1)}), bf16[128,2,896]{2,1,0:T(2,128)(2,1)S(1)}, u32[]{:S(2)}, u32[]{:S(2)}) async-start(bf16[128,2,896]{2,1,0:T(2,128)(2,1)} %get-tuple-element.56), calls=%async_computation.2 | async-start | bytes 917504 | tf_op jit(solution)/shard_map/all_to_all | solution.py:298
  35.8 2.6 %collective-permute-start.4 = (bf16[128,1536]{1,0:T(8,128)(2,1)S(1)}, bf16[128,1536]{1,0:T(8,128)(2,1)S(1)}, u32[]{:S(2)}, u32[]{:S(2)}) collective-permute-start(bf16[128,1536]{1,0:T(8,128)(2,1)S(1)} %constant_dynamic-update-slice_fusion.2.refs_1_), channel_id=1, source_target_pairs={{0,1},{1,0},{2,3},{3,2},{4,5},{5,4},{6,7},{7,6},{8,9},{9,8},{10,11... | collective-permute-start | bytes 1179656 | tf_op jit(solution)/shard_map/ppermute | solution.py:302
